TPU v7x, 32 devices: a whole 2x2x4 slice. The times are simulated.
32 devices in a mesh: row: 8 (over y, x, core), col: 4 (over z).
Axes of the slice: x: 2, y: 2, z: 4, core: 2. Of those that a mesh axis runs over, the one named last changes fastest.
Arguments:
- tokens: bfloat16 [128, 12288], P('col', 'row'), may hold values from -6 to 6
- cotangent: bfloat16 [128, 12288], P('col', 'row'), may hold values from -1.5 to 1.5
- w_in: bfloat16 [12288, 24576], P('row', 'col'), may hold values from -0.0546875 to 0.0546875
- w_out: bfloat16 [24576, 12288], P('col', 'row'), may hold values from -0.0390625 to 0.0390625
Outputs:
- layer_out: bfloat16 [128, 12288], P('col', 'row')
- grad_tokens: bfloat16 [128, 12288], P('col', 'row')
- grad_w_in: bfloat16 [12288, 24576], P('row', 'col')
- grad_w_out: bfloat16 [24576, 12288], P('col', 'row')
All inputs are finite; a program needn't handle non-finite values.
Results may differ from a plain program's by a relative error of at most 0.034.
Values may be sent and summed in bfloat16 or wider, within the bound.
No kernel may reach another device: no remote copies, remote signals or barrier semaphores. Data moves between devices by JAX's collectives and lax.ppermute only.
A program may use at most 128 MiB of HBM per device.

v0:
```python
import jax
import jax.numpy as jnp
from jax import lax
from jax.sharding import PartitionSpec as P


def gelu_fn(value):
    return jax.nn.gelu(value, approximate=True)


def gelu_back(hidden, grad_act):
    unused, pullback = jax.vjp(gelu_fn, hidden)
    return pullback(grad_act)[0].astype(jnp.bfloat16)


def shards(tokens, cotangent, w_in, w_out):
    token_full, cot_full = (
        lax.all_gather(tokens, "col", axis=0, tiled=True),
        lax.all_gather(cotangent, "col", axis=0, tiled=True),
    )
    block = token_full
    hidden_share = lax.psum_scatter(
        jnp.dot(block, w_in, preferred_element_type=jnp.float32).astype(jnp.bfloat16),
        "row",
        scatter_dimension=0,
        tiled=True,
    ).astype(jnp.float32)
    act_share = gelu_fn(hidden_share).astype(jnp.bfloat16)
    act = lax.all_gather(act_share, "row", axis=0, tiled=True)
    block = act
    layer_out = lax.psum_scatter(
        jnp.dot(block, w_out, preferred_element_type=jnp.float32).astype(jnp.bfloat16),
        "col",
        scatter_dimension=0,
        tiled=True,
    )
    block = cot_full
    grad_share = lax.psum_scatter(
        lax.dot_general(
            block, w_out, (((1,), (1,)), ((), ())), preferred_element_type=jnp.float32
        ).astype(jnp.bfloat16),
        "row",
        scatter_dimension=0,
        tiled=True,
    ).astype(jnp.float32)
    grad_hidden_share = gelu_back(hidden_share, grad_share)
    grad_hidden = lax.all_gather(grad_hidden_share, "row", axis=0, tiled=True)
    grad_w_out = lax.dot_general(
        act, cot_full, (((0,), (0,)), ((), ())), preferred_element_type=jnp.float32
    ).astype(jnp.bfloat16)
    grad_w_in = lax.dot_general(
        token_full, grad_hidden, (((0,), (0,)), ((), ())), preferred_element_type=jnp.float32
    ).astype(jnp.bfloat16)
    block = grad_hidden
    grad_tokens = lax.psum_scatter(
        lax.dot_general(
            block, w_in, (((1,), (1,)), ((), ())), preferred_element_type=jnp.float32
        ).astype(jnp.bfloat16),
        "col",
        scatter_dimension=0,
        tiled=True,
    )
    return (layer_out, grad_tokens, grad_w_in, grad_w_out)


def solution(mesh):
    return jax.shard_map(
        shards,
        mesh=mesh,
        in_specs=(P("col", "row"), P("col", "row"), P("row", "col"), P("col", "row")),
        out_specs=(P("col", "row"), P("col", "row"), P("row", "col"), P("col", "row")),
        check_vma=False,
    )
```

profile of v0, /device:TPU:0, one launch (start us, length us, event | category | flops | bytes accessed | tf_op | source)
XLA Modules:
  0.0 253.1 jit_solution(8012047769377305376)
XLA Ops:
  7.2 0.0 reduce-scatter.9.cloned.1.call-start
  7.2 16.4 %all_gather.14 = bf16[128,1536]{1,0:T(8,128)(2,1)S(1)} all-gather(bf16[32,1536]{1,0:T(8,128)(2,1)} %param.5), channel_id=1, replica_groups=mesh['row'=8,'col'=4] {'col'}, dimensions={0}, use_global_device_ids=true | all-gather | bytes 491520 | tf_op jit(solution)/shard_map/all_gather | solution.py:19
  23.7 13.7 %convolution_convert_fusion.2 = bf16[128,6144]{1,0:T(8,128)(2,1)} fusion(bf16[128,1536]{1,0:T(8,128)(2,1)S(1)} %all_gather.14, bf16[6144,1536]{1,0:T(8,128)(2,1)} %param.7), kind=kOutput, calls=%fused_computation.3 | convolution fusion | flops 2416705536 | bytes 20840448 | tf_op jit(solution)/shard_map/dot_general | solution.py:39
  37.4 0.0 reduce-scatter.9.cloned.1.call-update
  37.4 0.0 reduce-scatter.5.cloned.1.call-start
  37.4 15.5 %all_gather.12 = bf16[128,1536]{1,0:T(8,128)(2,1)S(1)} all-gather(bf16[32,1536]{1,0:T(8,128)(2,1)S(1)} %copy-done.2), channel_id=1, replica_groups=mesh['row'=8,'col'=4] {'col'}, dimensions={0}, use_global_device_ids=true | all-gather | bytes 491520 | tf_op jit(solution)/shard_map/all_gather | solution.py:18
  52.9 10.1 %convolution_convert_fusion.3 = bf16[128,6144]{1,0:T(8,128)(2,1)} fusion(bf16[128,1536]{1,0:T(8,128)(2,1)S(1)} %all_gather.12, bf16[1536,6144]{1,0:T(8,128)(2,1)} %param.6), kind=kOutput, calls=%fused_computation.4 | convolution fusion | flops 2416705536 | bytes 20840448 | tf_op jit(solution)/shard_map/dot_general | solution.py:23
  63.0 0.0 all-gather.3.cloned.1.call-start
  63.1 14.7 %reduce-scatter.9.cloned.1.call-done = bf16[16,6144]{1,0:T(8,128)(2,1)} async-done(((bf16[128,6144]{1,0:T(8,128)(2,1)}), bf16[16,6144]{1,0:T(8,128)(2,1)}) %reduce-scatter.9.cloned.1.call-update) | async-done | bytes 196624 | tf_op jit(solution)/shard_map/reduce_scatter | solution.py:38
  77.8 42.4 %reduce-scatter.5.cloned.1.call-done = bf16[16,6144]{1,0:T(8,128)(2,1)} async-done(((bf16[128,6144]{1,0:T(8,128)(2,1)}), bf16[16,6144]{1,0:T(8,128)(2,1)}) %reduce-scatter.5.cloned.1.call-update) | async-done | bytes 196624 | tf_op jit(solution)/shard_map/reduce_scatter | solution.py:22
  120.1 2.1 fusion.4
  122.2 0.0 all-gather.3.cloned.1.call-update
  122.2 0.0 all-gather.5.cloned.1.call-start
  122.3 0.5 all-gather.5.cloned.1.call-update
  122.8 0.0 reduce-scatter.7.cloned.1.call-start
  122.9 25.4 %all-gather.3.cloned.1.call-done = bf16[128,6144]{1,0:T(8,128)(2,1)} async-done(((bf16[16,6144]{1,0:T(8,128)(2,1)}), bf16[128,6144]{1,0:T(8,128)(2,1)}) %all-gather.3.cloned.1.call-update) | async-done | bytes 1572880 | tf_op jit(solution)/shard_map/all_gather | solution.py:29
  148.3 10.2 %convolution_convert_fusion.5 = bf16[128,1536]{1,0:T(8,128)(2,1)} fusion(bf16[128,6144]{1,0:T(8,128)(2,1)} %all-gather.3.cloned.1.call-done, bf16[6144,1536]{1,0:T(8,128)(2,1)} %param.7), kind=kOutput, calls=%fused_computation.6 | convolution fusion | flops 2416115712 | bytes 20840448 | tf_op jit(solution)/shard_map/dot_general | solution.py:32
  158.5 0.2 reduce-scatter.11.cloned.1.call-start
  158.8 17.6 %all-gather.5.cloned.1.call-done = bf16[128,6144]{1,0:T(8,128)(2,1)} async-done(((bf16[16,6144]{1,0:T(8,128)(2,1)}), bf16[128,6144]{1,0:T(8,128)(2,1)}) %all-gather.5.cloned.1.call-update) | async-done | bytes 1572880 | tf_op jit(solution)/shard_map/all_gather | solution.py:47
  176.3 10.9 %fusion = bf16[1536,6144]{0,1:T(8,128)(2,1)} fusion(bf16[128,6144]{1,0:T(8,128)(2,1)} %all-gather.5.cloned.1.call-done, bf16[128,1536]{1,0:T(8,128)(2,1)S(1)} %all_gather.12), kind=kOutput, calls=%fused_computation.2 | convolution fusion | flops 2425356288 | bytes 20840448 | tf_op jit(solution)/shard_map/dot_general | solution.py:51
  187.2 24.7 %copy.8 = bf16[1536,6144]{1,0:T(8,128)(2,1)} copy(bf16[1536,6144]{0,1:T(8,128)(2,1)} %fusion) | data formatting | bytes 37748736
  212.0 13.5 %convolution_convert_fusion.4 = bf16[128,1536]{1,0:T(8,128)(2,1)} fusion(bf16[128,6144]{1,0:T(8,128)(2,1)S(1)} %copy-done.1, bf16[1536,6144]{1,0:T(8,128)(2,1)} %param.6), kind=kOutput, calls=%fused_computation.5 | convolution fusion | flops 2416115712 | bytes 20840448 | tf_op jit(solution)/shard_map/dot_general | solution.py:56
  225.5 9.5 %convolution_convert_fusion = bf16[6144,1536]{1,0:T(8,128)(2,1)} fusion(bf16[128,6144]{1,0:T(8,128)(2,1)S(1)} %copy-done, bf16[128,1536]{1,0:T(8,128)(2,1)S(1)} %all_gather.14), kind=kOutput, calls=%fused_computation | convolution fusion | flops 2425356288 | bytes 20840448 | tf_op jit(solution)/shard_map/dot_general | solution.py:48
  235.1 11.2 %reduce-scatter.11.cloned.1.call-done = bf16[32,1536]{1,0:T(8,128)(2,1)} async-done(((bf16[128,1536]{1,0:T(8,128)(2,1)}), bf16[32,1536]{1,0:T(8,128)(2,1)}) %reduce-scatter.11.cloned.1.call-update) | async-done | bytes 98320 | tf_op jit(solution)/shard_map/reduce_scatter | solution.py:55
  (10 shorter events, 0.1 us)
Async XLA Ops:
  7.2 30.3 %copy-start.2 = (bf16[32,1536]{1,0:T(8,128)(2,1)S(1)}, bf16[32,1536]{1,0:T(8,128)(2,1)}, u32[]{:S(2)}) copy-start(bf16[32,1536]{1,0:T(8,128)(2,1)} %param.4) | copy-start | bytes 294916
  7.2 70.6 %reduce-scatter.9.cloned.1.call-start = ((), (), s32[]{:S(2)}) async-start(), calls=%async_computation.7 | async-start | bytes 1769472 | tf_op jit(solution)/shard_map/reduce_scatter | solution.py:38
  37.4 82.8 %reduce-scatter.5.cloned.1.call-start = ((), (), s32[]{:S(2)}) async-start(), calls=%async_computation.4 | async-start | bytes 1769472 | tf_op jit(solution)/shard_map/reduce_scatter | solution.py:22
  63.0 85.2 %all-gather.3.cloned.1.call-start = ((), (), s32[]{:S(2)}) async-start(), calls=%async_computation.5 | async-start | bytes 1769472 | tf_op jit(solution)/shard_map/all_gather | solution.py:29
  122.2 54.1 %all-gather.5.cloned.1.call-start = ((), (), s32[]{:S(2)}) async-start(), calls=%async_computation.8 | async-start | bytes 1769472 | tf_op jit(solution)/shard_map/all_gather | solution.py:47
  122.8 112.2 %reduce-scatter.7.cloned.1.call-start = ((), (), s32[]{:S(2)}) async-start(), calls=%async_computation.6 | async-start | bytes 491520 | tf_op jit(solution)/shard_map/reduce_scatter | solution.py:31
  158.5 87.7 %reduce-scatter.11.cloned.1.call-start = ((), (), s32[]{:S(2)}) async-start(), calls=%async_computation.9 | async-start | bytes 491520 | tf_op jit(solution)/shard_map/reduce_scatter | solution.py:55
  187.2 24.7 %copy-start.1 = (bf16[128,6144]{1,0:T(8,128)(2,1)S(1)}, bf16[128,6144]{1,0:T(8,128)(2,1)}, u32[]{:S(2)}) copy-start(bf16[128,6144]{1,0:T(8,128)(2,1)} %all-gather.5.cloned.1.call-done) | copy-start | bytes 4718596
  212.0 13.6 %copy-start = (bf16[128,6144]{1,0:T(8,128)(2,1)S(1)}, bf16[128,6144]{1,0:T(8,128)(2,1)}, u32[]{:S(2)}) copy-start(bf16[128,6144]{1,0:T(8,128)(2,1)} %all-gather.3.cloned.1.call-done) | copy-start | bytes 4718596
Sparse Core Ops, SparseCore 0:
  37.5 40.2 reduce-scatter.8
  81.6 38.4 reduce-scatter.4
  122.6 25.6 all-gather.2
  150.6 25.6 all-gather.4
  179.0 20.6 reduce-scatter.6
  225.7 20.5 reduce-scatter.10
where the time goes:
time: 254 us; the launch traced here: 253 us
  waiting for transfers between devices  112 us (44%)
  matrix products  68 us (27%)
  blocking collectives  31.9 us (13%)
  local copies, waits for them, and re-layouts  24.7 us (10%)
  between operations  14.1 us (6%)
    reduce_scatter x1, waiting for transfers between devices, shards(): lax.psum_scatter(jnp.dot(block, w_in, preferred_element_type=jnp.float32)...  42.4 us
    all_gather x1, waiting for transfers between devices, shards(): act = lax.all_gather(act_share, 'row', axis=0, tiled=True)  25.4 us
    unnamed x7, local copies, waits for them, and re-layouts  24.7 us
    all_gather x1, waiting for transfers between devices, shards(): grad_hidden = lax.all_gather(grad_hidden_share, 'row', axis=0, tiled=True)  17.6 us
    all_gather x1, blocking collectives, shards(): lax.all_gather(cotangent, 'col', axis=0, tiled=True)  16.4 us
    all_gather x1, blocking collectives, shards(): lax.all_gather(tokens, 'col', axis=0, tiled=True)  15.5 us
    reduce_scatter x1, waiting for transfers between devices, shards(): lax.psum_scatter(lax.dot_general(block, w_out, (((1,), (1,)), ((), ())),...  14.7 us
    dot_general x1, matrix products, shards(): lax.dot_general(block, w_out, (((1,), (1,)), ((), ())), preferred_element...  13.7 us
  transfers between devices with their start and end apart: 6, of which 5 were waited for; matrix products, arithmetic and copies ran while one was open for 31% of the time, Pallas kernels for 0%

commit v1 on v0

v1 whole, which is shorter than its diff:
```python
import functools

import jax
import jax.numpy as jnp
from jax import lax
from jax.experimental import pallas as pl
from jax.experimental.pallas import tpu as pltpu
from jax.sharding import PartitionSpec as P

BF16 = jnp.bfloat16
F32 = jnp.float32
MIB = 1024 * 1024
VMEM_LIMIT = 48 * MIB


def gelu_fn(value):
    return jax.nn.gelu(value, approximate=True)


def gelu_back(hidden, grad_act):
    unused, pullback = jax.vjp(gelu_fn, hidden)
    return pullback(grad_act)[0].astype(BF16)


def swap(value, axis, flip, count):
    return lax.ppermute(value, axis, [(i, i ^ flip) for i in range(count)])


def dot(left, right, left_dim, right_dim):
    return lax.dot_general(
        left, right, (((left_dim,), (right_dim,)), ((), ())), preferred_element_type=F32
    )


def whole():
    return pl.BlockSpec(memory_space=pltpu.VMEM)


def project_kernel(count, right_dim, me_ref, *refs):
    pieces, (w_ref, keep_ref, send_ref, left) = refs[:count], refs[count:]
    step = pl.program_id(0)

    @pl.when(step == 0)
    def _():
        size = pieces[0].shape[0]
        for i, piece in enumerate(pieces):
            left[i * size : (i + 1) * size, :] = piece[...]

    out = dot(left[...], w_ref[...], 1, right_dim).astype(BF16)

    @pl.when(step % 2 == 0)
    def _():
        keep_ref[0] = out

    @pl.when(step % 2 == 1)
    def _():
        send_ref[0] = out


def project(me, pieces, weight, rows, by_rows):
    tokens = len(pieces) * pieces[0].shape[0]
    width = pieces[0].shape[1]
    hidden = weight.shape[0 if by_rows else 1]
    block = hidden // rows
    if by_rows:
        w_spec = pl.BlockSpec((block, width), lambda s, me: (me[0] ^ s, 0))
    else:
        w_spec = pl.BlockSpec((width, block), lambda s, me: (0, me[0] ^ s))
    out = jax.ShapeDtypeStruct((rows // 2, tokens, block), BF16)
    out_spec = pl.BlockSpec((1, tokens, block), lambda s, me: (s // 2, 0, 0))
    return pl.pallas_call(
        functools.partial(project_kernel, len(pieces), 1 if by_rows else 0),
        grid_spec=pltpu.PrefetchScalarGridSpec(
            num_scalar_prefetch=1,
            grid=(rows,),
            in_specs=[whole()] * len(pieces) + [w_spec],
            out_specs=[out_spec, out_spec],
            scratch_shapes=[pltpu.VMEM((tokens, width), BF16)],
        ),
        out_shape=[out, out],
        compiler_params=pltpu.CompilerParams(vmem_limit_bytes=VMEM_LIMIT),
        cost_estimate=pl.CostEstimate(
            flops=2 * tokens * width * hidden,
            bytes_accessed=2 * width * hidden + 2 * tokens * (width + hidden),
            transcendentals=0,
        ),
    )(me, *pieces, weight)


def back_kernel(rows, cols, by_rows, me_ref, *refs):
    blocks, refs = refs[:rows], refs[rows:]
    others, refs = refs[:cols], refs[cols:]
    w_ref, out_ref, grad_ref, act, other, total = refs
    step = pl.program_id(0)

    @pl.when(step == 0)
    def _():
        for i, block in enumerate(blocks):
            act[i] = block[...]
        size = others[0].shape[0]
        for i, piece in enumerate(others):
            other[i * size : (i + 1) * size, :] = piece[...]
        total[...] = jnp.zeros_like(total)

    value = act[step]
    total[...] += dot(value, w_ref[...], 1, 0 if by_rows else 1)
    if by_rows:
        grad_ref[...] = dot(value, other[...], 0, 0).astype(BF16)
    else:
        grad_ref[...] = dot(other[...], value, 0, 0).astype(BF16)

    @pl.when(step == rows - 1)
    def _():
        size = others[0].shape[0]
        for i in range(cols):
            out_ref[i] = total[i * size : (i + 1) * size, :].astype(BF16)


def back(me, blocks, others, weight, by_rows):
    rows, cols = len(blocks), len(others)
    tokens, block = blocks[0].shape
    size, width = others[0].shape
    hidden = rows * block
    if by_rows:
        w_spec = pl.BlockSpec((block, width), lambda s, me: (me[0] ^ s, 0))
    else:
        w_spec = pl.BlockSpec((width, block), lambda s, me: (0, me[0] ^ s))
    return pl.pallas_call(
        functools.partial(back_kernel, rows, cols, by_rows),
        grid_spec=pltpu.PrefetchScalarGridSpec(
            num_scalar_prefetch=1,
            grid=(rows,),
            in_specs=[whole()] * (rows + cols) + [w_spec],
            out_specs=[whole(), w_spec],
            scratch_shapes=[
                pltpu.VMEM((rows, tokens, block), BF16),
                pltpu.VMEM((tokens, width), BF16),
                pltpu.VMEM((tokens, width), F32),
            ],
        ),
        out_shape=[
            jax.ShapeDtypeStruct((cols, size, width), BF16),
            jax.ShapeDtypeStruct(weight.shape, BF16),
        ],
        compiler_params=pltpu.CompilerParams(vmem_limit_bytes=VMEM_LIMIT),
        cost_estimate=pl.CostEstimate(
            flops=4 * tokens * width * hidden,
            bytes_accessed=4 * width * hidden + 2 * tokens * (2 * width + hidden),
            transcendentals=0,
        ),
    )(me, *blocks, *others, weight)


def gather_col(piece, cols):
    return [piece] + [swap(piece, "col", q, cols) for q in range(1, cols)]


def scatter_row(keep, send, rows):
    got = swap(send, "row", 1, rows)
    pair = [keep[i].astype(F32) + got[i].astype(F32) for i in range(rows // 2)]
    total = pair[0]
    for i in range(1, rows // 2):
        total = total + swap(pair[i].astype(BF16), "row", 2 * i, rows).astype(F32)
    return total


def gather_row(share, rows):
    own = [share] + [swap(share, "row", 2 * i, rows) for i in range(1, rows // 2)]
    blocks = []
    for value in own:
        blocks += [value, swap(value, "row", 1, rows)]
    return blocks


def scatter_col(parts, cols):
    total = parts[0].astype(F32)
    for q in range(1, cols):
        total = total + swap(parts[q], "col", q, cols).astype(F32)
    return total.astype(BF16)


def blocked(rows, cols, tokens, cotangent, w_in, w_out):
    me = lax.axis_index("row").astype(jnp.int32).reshape(1)
    token_pieces = gather_col(tokens, cols)
    cot_pieces = gather_col(cotangent, cols)
    hidden = scatter_row(*project(me, token_pieces, w_in, rows, False), rows)
    grad_act = scatter_row(*project(me, cot_pieces, w_out, rows, True), rows)
    act = gather_row(gelu_fn(hidden).astype(BF16), rows)
    layer_parts, grad_w_out = back(me, act, cot_pieces, w_out, True)
    grad_hidden = gather_row(gelu_back(hidden, grad_act), rows)
    token_parts, grad_w_in = back(me, grad_hidden, token_pieces, w_in, False)
    layer_out = scatter_col(layer_parts, cols)
    grad_tokens = scatter_col(token_parts, cols)
    return (layer_out, grad_tokens, grad_w_in, grad_w_out)


def collective(tokens, cotangent, w_in, w_out):
    token_full = lax.all_gather(tokens, "col", axis=0, tiled=True)
    cot_full = lax.all_gather(cotangent, "col", axis=0, tiled=True)

    def over(value, axis):
        return lax.psum_scatter(value.astype(BF16), axis, scatter_dimension=0, tiled=True)

    hidden = over(dot(token_full, w_in, 1, 0), "row").astype(F32)
    grad_act = over(dot(cot_full, w_out, 1, 1), "row").astype(F32)
    act = lax.all_gather(gelu_fn(hidden).astype(BF16), "row", axis=0, tiled=True)
    grad_hidden = lax.all_gather(gelu_back(hidden, grad_act), "row", axis=0, tiled=True)
    layer_out = over(dot(act, w_out, 1, 0), "col")
    grad_tokens = over(dot(grad_hidden, w_in, 1, 1), "col")
    grad_w_in = dot(token_full, grad_hidden, 0, 0).astype(BF16)
    grad_w_out = dot(act, cot_full, 0, 0).astype(BF16)
    return (layer_out, grad_tokens, grad_w_in, grad_w_out)


def solution(mesh):
    rows, cols = mesh.shape["row"], mesh.shape["col"]

    def shards(tokens, cotangent, w_in, w_out):
        powers = rows & (rows - 1) == 0 and cols & (cols - 1) == 0
        if powers and rows > 1 and w_in.shape[1] % (rows * 128) == 0:
            return blocked(rows, cols, tokens, cotangent, w_in, w_out)
        return collective(tokens, cotangent, w_in, w_out)

    return jax.shard_map(
        shards,
        mesh=mesh,
        in_specs=(P("col", "row"), P("col", "row"), P("row", "col"), P("col", "row")),
        out_specs=(P("col", "row"), P("col", "row"), P("row", "col"), P("col", "row")),
        check_vma=False,
    )
```

time: 254 us -> 141 us (0.56)
  waiting for transfers between devices: 112 us -> 34.3 us
  matrix products: 68 us -> 0 us
  Pallas kernels: 0 us -> 59.7 us
  starting transfers between devices: 0.42 us -> 42 us
  blocking collectives: 31.9 us -> 0 us
  local copies, waits for them, and re-layouts: 24.7 us -> 0.94 us
  between operations: 14.1 us -> 0.76 us
    reduce_scatter x4 -> x0, waiting for transfers between devices: 68.3 us -> none  [the longest x1 42.4 us: shards(): lax.psum_scatter(jnp.dot(block, w_in, preferred_element_type=jnp.float32)...]
    dot_general x6 -> x0, matrix products: 68 us -> none  [the longest x1 13.7 us: shards(): lax.dot_general(block, w_out, (((1,), (1,)), ((), ())), preferred_element...]
    pallas_call x0 -> x4, Pallas kernels: none -> 59.7 us  [the longest x2 38 us: back(): pl.pallas_call(functools.partial(back_kernel, rows, cols, by_rows), grid_...]
    all_gather x2 -> x0, waiting for transfers between devices: 43 us -> none  [the longest x1 25.4 us: shards(): act = lax.all_gather(act_share, 'row', axis=0, tiled=True)]
    ppermute x0 -> x34, starting transfers between devices: none -> 42 us  [swap(): return lax.ppermute(value, axis, [(i, i ^ flip) for i in range(count)])]
    ppermute x0 -> x34, waiting for transfers between devices: none -> 34.3 us  [swap(): return lax.ppermute(value, axis, [(i, i ^ flip) for i in range(count)])]
    all_gather x2 -> x0, blocking collectives: 31.9 us -> none  [the longest x1 16.4 us: shards(): lax.all_gather(cotangent, 'col', axis=0, tiled=True)]
    unnamed x7 -> x6, local copies, waits for them, and re-layouts: 24.7 us -> 0.9 us
  transfers between devices with their start and end apart: 6 -> 34, of which waited for: 5 -> 15; matrix products, arithmetic and copies ran while one was open for 31% -> 1% of each run, Pallas kernels for 0% -> 43%
where the time goes in v1:
time: 141 us; the launch traced here: 140 us
  Pallas kernels  59.7 us (42%)
  starting transfers between devices  42 us (30%)
  waiting for transfers between devices  34.3 us (24%)
  other arithmetic  2.19 us (2%)
    ppermute x34, starting transfers between devices, swap(): return lax.ppermute(value, axis, [(i, i ^ flip) for i in range(count)])  42 us
    pallas_call x2, Pallas kernels, back(): pl.pallas_call(functools.partial(back_kernel, rows, cols, by_rows), grid_...  38 us
    ppermute x34, waiting for transfers between devices, swap(): return lax.ppermute(value, axis, [(i, i ^ flip) for i in range(count)])  34.3 us
    pallas_call x2, Pallas kernels, project(): pl.pallas_call(functools.partial(project_kernel, len(pieces), 1 if by_row...  21.7 us
  transfers between devices with their start and end apart: 34, of which 15 were waited for; matrix products, arithmetic and copies ran while one was open for 1% of the time, Pallas kernels for 43%

profile of v1, /device:TPU:0, one launch (start us, length us, event | category | flops | bytes accessed | tf_op | source)
XLA Modules:
  0.0 139.9 jit_solution(7361639489099492466)
XLA Ops:
  0.6 5.1 %collective-permute-start.16 = (bf16[32,1536]{1,0:T(8,128)(2,1)}, bf16[32,1536]{1,0:T(8,128)(2,1)S(1)}, u32[]{:S(2)}, u32[]{:S(2)}) collective-permute-start(bf16[32,1536]{1,0:T(8,128)(2,1)} %refs_0_.3), channel_id=1, source_target_pairs={{0,3},{1,2},{2,1},{3,0},{4,7},{5,6},{6,5},{7,4},{8,11},{9,10},{10,... | collective-permute-start | bytes 294920 | tf_op jit(solution)/shard_map/ppermute | solution.py:26
  6.4 3.7 %collective-permute-start.2 = (bf16[32,1536]{1,0:T(8,128)(2,1)}, bf16[32,1536]{1,0:T(8,128)(2,1)S(1)}, u32[]{:S(2)}, u32[]{:S(2)}) collective-permute-start(bf16[32,1536]{1,0:T(8,128)(2,1)} %refs_8_.3), channel_id=1, source_target_pairs={{0,3},{1,2},{2,1},{3,0},{4,7},{5,6},{6,5},{7,4},{8,11},{9,10},{10,... | collective-permute-start | bytes 294920 | tf_op jit(solution)/shard_map/ppermute | solution.py:26
  10.1 6.7 %collective-permute-start = (bf16[32,1536]{1,0:T(8,128)(2,1)}, bf16[32,1536]{1,0:T(8,128)(2,1)S(1)}, u32[]{:S(2)}, u32[]{:S(2)}) collective-permute-start(bf16[32,1536]{1,0:T(8,128)(2,1)} %refs_8_.3), channel_id=1, source_target_pairs={{0,1},{1,0},{2,3},{3,2},{4,5},{5,4},{6,7},{7,6},{8,9},{9,8},{10,11... | collective-permute-start | bytes 294920 | tf_op jit(solution)/shard_map/ppermute | solution.py:26
  16.9 2.5 %collective-permute-done.15.refs_10_.refs_2_ = bf16[32,1536]{1,0:T(8,128)(2,1)S(1)} collective-permute-done((bf16[32,1536]{1,0:T(8,128)(2,1)}, bf16[32,1536]{1,0:T(8,128)(2,1)S(1)}, u32[]{:S(2)}, u32[]{:S(2)}) %collective-permute-start.15) | collective-permute-done | bytes 98336 | tf_op jit(solution)/shard_map/ppermute | solution.py:26
  20.3 11.7 %shard_map.77 = (bf16[4,128,768]{2,1,0:T(8,128)(2,1)S(1)}, bf16[4,128,768]{2,1,0:T(8,128)(2,1)S(1)}) custom-call(s32[1]{0:T(128)} %bitcast.me_ref, bf16[32,1536]{1,0:T(8,128)(2,1)S(1)} %copy-done, bf16[32,1536]{1,0:T(8,128)(2,1)S(1)} %collective-permute-done.14.refs_9_.refs_1_, bf16[32,1536]{1,0:T(8,128)(2,1)S(1)} %collective-permute-done.15.refs_10_.refs_2_, ...), custom_call_target="tpu_custom_call" | custom-call | flops 2415919104 | bytes 20840448 | tf_op jit(solution)/shard_map/pallas_call | solution.py:71
  32.1 10.0 %shard_map.75 = (bf16[4,128,768]{2,1,0:T(8,128)(2,1)S(1)}, bf16[4,128,768]{2,1,0:T(8,128)(2,1)S(1)}) custom-call(s32[1]{0:T(128)} %bitcast.me_ref, bf16[32,1536]{1,0:T(8,128)(2,1)S(1)} %copy-done.2, bf16[32,1536]{1,0:T(8,128)(2,1)S(1)} %collective-permute-done.refs_1_.refs_9_, bf16[32,1536]{1,0:T(8,128)(2,1)S(1)} %collective-permute-done.1.refs_2_.refs_10_, ...), custom_call_target="tpu_custom_call" | custom-call | flops 2415919104 | bytes 20840448 | tf_op jit(solution)/shard_map/pallas_call | solution.py:71
  42.8 1.6 %collective-permute-start.21 = (bf16[128,768]{1,0:T(8,128)(2,1)S(1)}, bf16[128,768]{1,0:T(8,128)(2,1)S(1)}, u32[]{:S(2)}, u32[]{:S(2)}) collective-permute-start(bf16[128,768]{1,0:T(8,128)(2,1)S(1)} %get-tuple-element.22), channel_id=1, source_target_pairs={{0,8},{4,12},{8,0},{12,4},{16,24},{20,28},{24,16},{28,20},{1,9},{5... | collective-permute-start | bytes 589832 | tf_op jit(solution)/shard_map/ppermute | solution.py:26
  46.5 1.6 %collective-permute-start.4 = (bf16[128,768]{1,0:T(8,128)(2,1)S(1)}, bf16[128,768]{1,0:T(8,128)(2,1)S(1)}, u32[]{:S(2)}, u32[]{:S(2)}) collective-permute-start(bf16[128,768]{1,0:T(8,128)(2,1)S(1)} %get-tuple-element.25), channel_id=1, source_target_pairs={{0,8},{4,12},{8,0},{12,4},{16,24},{20,28},{24,16},{28,20},{1,9},{5... | collective-permute-start | bytes 589832 | tf_op jit(solution)/shard_map/ppermute | solution.py:26
  50.6 1.5 %collective-permute-start.5 = (bf16[128,768]{1,0:T(8,128)(2,1)S(1)}, bf16[128,768]{1,0:T(8,128)(2,1)S(1)}, u32[]{:S(2)}, u32[]{:S(2)}) collective-permute-start(bf16[128,768]{1,0:T(8,128)(2,1)S(1)} %get-tuple-element.27), channel_id=1, source_target_pairs={{0,16},{4,20},{8,24},{12,28},{16,0},{20,4},{24,8},{28,12},{1,17},{... | collective-permute-start | bytes 589832 | tf_op jit(solution)/shard_map/ppermute | solution.py:26
  52.1 3.7 %collective-permute-done.23 = bf16[128,768]{1,0:T(8,128)(2,1)S(1)} collective-permute-done((bf16[128,768]{1,0:T(8,128)(2,1)S(1)}, bf16[128,768]{1,0:T(8,128)(2,1)S(1)}, u32[]{:S(2)}, u32[]{:S(2)}) %collective-permute-start.23) | collective-permute-done | bytes 196640 | tf_op jit(solution)/shard_map/ppermute | solution.py:26
  55.8 1.9 %collective-permute-done.22 = bf16[128,768]{1,0:T(8,128)(2,1)S(1)} collective-permute-done((bf16[128,768]{1,0:T(8,128)(2,1)S(1)}, bf16[128,768]{1,0:T(8,128)(2,1)S(1)}, u32[]{:S(2)}, u32[]{:S(2)}) %collective-permute-start.22) | collective-permute-done | bytes 196640 | tf_op jit(solution)/shard_map/ppermute | solution.py:26
  59.1 4.3 %collective-permute-done.6 = bf16[128,768]{1,0:T(8,128)(2,1)S(1)} collective-permute-done((bf16[128,768]{1,0:T(8,128)(2,1)S(1)}, bf16[128,768]{1,0:T(8,128)(2,1)S(1)}, u32[]{:S(2)}, u32[]{:S(2)}) %collective-permute-start.6) | collective-permute-done | bytes 196640 | tf_op jit(solution)/shard_map/ppermute | solution.py:26
  66.8 1.5 %collective-permute-start.27 = (bf16[128,768]{1,0:T(8,128)(2,1)S(1)}, bf16[128,768]{1,0:T(8,128)(2,1)S(1)}, u32[]{:S(2)}, u32[]{:S(2)}) collective-permute-start(bf16[128,768]{1,0:T(8,128)(2,1)S(1)} %get-tuple-element.20.refs_0_), channel_id=1, source_target_pairs={{0,16},{4,20},{8,24},{12,28},{16,0},{20,4},{24,8},{28,12},{1,17},{... | collective-permute-start | bytes 589832 | tf_op jit(solution)/shard_map/ppermute | solution.py:26
  68.8 1.5 %collective-permute-start.10 = (bf16[128,768]{1,0:T(8,128)(2,1)S(1)}, bf16[128,768]{1,0:T(8,128)(2,1)S(1)}, u32[]{:S(2)}, u32[]{:S(2)}) collective-permute-start(bf16[128,768]{1,0:T(8,128)(2,1)S(1)} %get-tuple-element.21.refs_0_), channel_id=1, source_target_pairs={{0,16},{4,20},{8,24},{12,28},{16,0},{20,4},{24,8},{28,12},{1,17},{... | collective-permute-start | bytes 589832 | tf_op jit(solution)/shard_map/ppermute | solution.py:26
  71.8 2.2 %collective-permute-done.29.refs_6_ = bf16[128,768]{1,0:T(8,128)(2,1)S(1)} collective-permute-done((bf16[128,768]{1,0:T(8,128)(2,1)S(1)}, bf16[128,768]{1,0:T(8,128)(2,1)S(1)}, u32[]{:S(2)}, u32[]{:S(2)}) %collective-permute-start.29) | collective-permute-done | bytes 196640 | tf_op jit(solution)/shard_map/ppermute | solution.py:26
  74.0 1.6 %collective-permute-start.25 = (bf16[128,768]{1,0:T(8,128)(2,1)S(1)}, bf16[128,768]{1,0:T(8,128)(2,1)S(1)}, u32[]{:S(2)}, u32[]{:S(2)}) collective-permute-start(bf16[128,768]{1,0:T(8,128)(2,1)S(1)} %get-tuple-element.20.refs_0_), channel_id=1, source_target_pairs={{0,8},{4,12},{8,0},{12,4},{16,24},{20,28},{24,16},{28,20},{1,9},{5... | collective-permute-start | bytes 589832 | tf_op jit(solution)/shard_map/ppermute | solution.py:26
  75.6 4.1 %collective-permute-done.27.refs_4_ = bf16[128,768]{1,0:T(8,128)(2,1)S(1)} collective-permute-done((bf16[128,768]{1,0:T(8,128)(2,1)S(1)}, bf16[128,768]{1,0:T(8,128)(2,1)S(1)}, u32[]{:S(2)}, u32[]{:S(2)}) %collective-permute-start.27) | collective-permute-done | bytes 196640 | tf_op jit(solution)/shard_map/ppermute | solution.py:26
  80.2 3.3 %collective-permute-done.10.refs_4_ = bf16[128,768]{1,0:T(8,128)(2,1)S(1)} collective-permute-done((bf16[128,768]{1,0:T(8,128)(2,1)S(1)}, bf16[128,768]{1,0:T(8,128)(2,1)S(1)}, u32[]{:S(2)}, u32[]{:S(2)}) %collective-permute-start.10) | collective-permute-done | bytes 196640 | tf_op jit(solution)/shard_map/ppermute | solution.py:26
  85.2 19.0 %shard_map.76 = (bf16[4,32,1536]{2,1,0:T(8,128)(2,1)S(1)}, bf16[6144,1536]{1,0:T(8,128)(2,1)}) custom-call(s32[1]{0:T(128)} %bitcast.me_ref, bf16[128,768]{1,0:T(8,128)(2,1)S(1)} %get-tuple-element.21.refs_0_, bf16[128,768]{1,0:T(8,128)(2,1)S(1)} %collective-permute-done.7.refs_1_, bf16[128,768]{1,0:T(8,128)(2,1)S(1)} %collective-permute-done.8.refs_2_, ...), custom_call_target="tpu_custom_call" | custom-call | flops 4831838208 | bytes 40108032 | tf_op jit(solution)/shard_map/pallas_call | solution.py:128
  104.3 2.7 %collective-permute-start.19 = (bf16[32,1536]{1,0:T(8,128)(2,1)S(1)}, bf16[32,1536]{1,0:T(8,128)(2,1)S(1)}, u32[]{:S(2)}, u32[]{:S(2)}) collective-permute-start(bf16[32,1536]{1,0:T(8,128)(2,1)S(1)} %get-tuple-element.32), channel_id=1, source_target_pairs={{0,3},{1,2},{2,1},{3,0},{4,7},{5,6},{6,5},{7,4},{8,11},{9,10},{10,... | collective-permute-start | bytes 294920 | tf_op jit(solution)/shard_map/ppermute | solution.py:26
  107.8 19.1 %shard_map.78 = (bf16[4,32,1536]{2,1,0:T(8,128)(2,1)S(1)}, bf16[1536,6144]{1,0:T(8,128)(2,1)}) custom-call(s32[1]{0:T(128)} %bitcast.me_ref, bf16[128,768]{1,0:T(8,128)(2,1)S(1)} %get-tuple-element.20.refs_0_, bf16[128,768]{1,0:T(8,128)(2,1)S(1)} %collective-permute-done.24.refs_1_, bf16[128,768]{1,0:T(8,128)(2,1)S(1)} %collective-permute-done.25.refs_2_, ...), custom_call_target="tpu_custom_call" | custom-call | flops 4831838208 | bytes 40108032 | tf_op jit(solution)/shard_map/pallas_call | solution.py:128
  127.9 2.7 %collective-permute-start.33 = (bf16[32,1536]{1,0:T(8,128)(2,1)S(1)}, bf16[32,1536]{1,0:T(8,128)(2,1)S(1)}, u32[]{:S(2)}, u32[]{:S(2)}) collective-permute-start(bf16[32,1536]{1,0:T(8,128)(2,1)S(1)} %get-tuple-element.29), channel_id=1, source_target_pairs={{0,3},{1,2},{2,1},{3,0},{4,7},{5,6},{6,5},{7,4},{8,11},{9,10},{10,... | collective-permute-start | bytes 294920 | tf_op jit(solution)/shard_map/ppermute | solution.py:26
  131.5 4.5 %collective-permute-done.33 = bf16[32,1536]{1,0:T(8,128)(2,1)S(1)} collective-permute-done((bf16[32,1536]{1,0:T(8,128)(2,1)S(1)}, bf16[32,1536]{1,0:T(8,128)(2,1)S(1)}, u32[]{:S(2)}, u32[]{:S(2)}) %collective-permute-start.33) | collective-permute-done | bytes 98336 | tf_op jit(solution)/shard_map/ppermute | solution.py:26
  136.1 3.2 %collective-permute-done.32 = bf16[32,1536]{1,0:T(8,128)(2,1)S(1)} collective-permute-done((bf16[32,1536]{1,0:T(8,128)(2,1)S(1)}, bf16[32,1536]{1,0:T(8,128)(2,1)S(1)}, u32[]{:S(2)}, u32[]{:S(2)}) %collective-permute-start.32) | collective-permute-done | bytes 98336 | tf_op jit(solution)/shard_map/ppermute | solution.py:26
  (61 shorter events, 19.5 us)
Async XLA Ops:
  0.6 9.5 %collective-permute-start.16 = (bf16[32,1536]{1,0:T(8,128)(2,1)}, bf16[32,1536]{1,0:T(8,128)(2,1)S(1)}, u32[]{:S(2)}, u32[]{:S(2)}) collective-permute-start(bf16[32,1536]{1,0:T(8,128)(2,1)} %refs_0_.3), channel_id=1, source_target_pairs={{0,3},{1,2},{2,1},{3,0},{4,7},{5,6},{6,5},{7,4},{8,11},{9,10},{10,... | collective-permute-start | bytes 294920 | tf_op jit(solution)/shard_map/ppermute | solution.py:26
  5.7 13.6 %collective-permute-start.15 = (bf16[32,1536]{1,0:T(8,128)(2,1)}, bf16[32,1536]{1,0:T(8,128)(2,1)S(1)}, u32[]{:S(2)}, u32[]{:S(2)}) collective-permute-start(bf16[32,1536]{1,0:T(8,128)(2,1)} %refs_0_.3), channel_id=1, source_target_pairs={{0,2},{1,3},{2,0},{3,1},{4,6},{5,7},{6,4},{7,5},{8,10},{9,11},{10,... | collective-permute-start | bytes 294920 | tf_op jit(solution)/shard_map/ppermute | solution.py:26
  5.7 13.6 %collective-permute-start.14 = (bf16[32,1536]{1,0:T(8,128)(2,1)}, bf16[32,1536]{1,0:T(8,128)(2,1)S(1)}, u32[]{:S(2)}, u32[]{:S(2)}) collective-permute-start(bf16[32,1536]{1,0:T(8,128)(2,1)} %refs_0_.3), channel_id=1, source_target_pairs={{0,1},{1,0},{2,3},{3,2},{4,5},{5,4},{6,7},{7,6},{8,9},{9,8},{10,11... | collective-permute-start | bytes 294920 | tf_op jit(solution)/shard_map/ppermute | solution.py:26
  6.4 25.7 %collective-permute-start.2 = (bf16[32,1536]{1,0:T(8,128)(2,1)}, bf16[32,1536]{1,0:T(8,128)(2,1)S(1)}, u32[]{:S(2)}, u32[]{:S(2)}) collective-permute-start(bf16[32,1536]{1,0:T(8,128)(2,1)} %refs_8_.3), channel_id=1, source_target_pairs={{0,3},{1,2},{2,1},{3,0},{4,7},{5,6},{6,5},{7,4},{8,11},{9,10},{10,... | collective-permute-start | bytes 294920 | tf_op jit(solution)/shard_map/ppermute | solution.py:26
  10.1 22.0 %collective-permute-start.1 = (bf16[32,1536]{1,0:T(8,128)(2,1)}, bf16[32,1536]{1,0:T(8,128)(2,1)S(1)}, u32[]{:S(2)}, u32[]{:S(2)}) collective-permute-start(bf16[32,1536]{1,0:T(8,128)(2,1)} %refs_8_.3), channel_id=1, source_target_pairs={{0,2},{1,3},{2,0},{3,1},{4,6},{5,7},{6,4},{7,5},{8,10},{9,11},{10,... | collective-permute-start | bytes 294920 | tf_op jit(solution)/shard_map/ppermute | solution.py:26
  10.1 22.0 %collective-permute-start = (bf16[32,1536]{1,0:T(8,128)(2,1)}, bf16[32,1536]{1,0:T(8,128)(2,1)S(1)}, u32[]{:S(2)}, u32[]{:S(2)}) collective-permute-start(bf16[32,1536]{1,0:T(8,128)(2,1)} %refs_8_.3), channel_id=1, source_target_pairs={{0,1},{1,0},{2,3},{3,2},{4,5},{5,4},{6,7},{7,6},{8,9},{9,8},{10,11... | collective-permute-start | bytes 294920 | tf_op jit(solution)/shard_map/ppermute | solution.py:26
  32.0 10.6 %collective-permute-start.20 = (bf16[4,128,768]{2,1,0:T(8,128)(2,1)S(1)}, bf16[4,128,768]{2,1,0:T(8,128)(2,1)S(1)}, u32[]{:S(2)}, u32[]{:S(2)}) collective-permute-start(bf16[4,128,768]{2,1,0:T(8,128)(2,1)S(1)} %get-tuple-element.16), channel_id=1, source_target_pairs={{0,4},{4,0},{8,12},{12,8},{16,20},{20,16},{24,28},{28,24},{1,5},{5... | collective-permute-start | bytes 2359304 | tf_op jit(solution)/shard_map/ppermute | solution.py:26
  44.3 11.5 %collective-permute-start.23 = (bf16[128,768]{1,0:T(8,128)(2,1)S(1)}, bf16[128,768]{1,0:T(8,128)(2,1)S(1)}, u32[]{:S(2)}, u32[]{:S(2)}) collective-permute-start(bf16[128,768]{1,0:T(8,128)(2,1)S(1)} %get-tuple-element.23), channel_id=1, source_target_pairs={{0,24},{4,28},{8,16},{12,20},{16,8},{20,12},{24,0},{28,4},{1,25},{... | collective-permute-start | bytes 589832 | tf_op jit(solution)/shard_map/ppermute | solution.py:26
  45.8 11.9 %collective-permute-start.22 = (bf16[128,768]{1,0:T(8,128)(2,1)S(1)}, bf16[128,768]{1,0:T(8,128)(2,1)S(1)}, u32[]{:S(2)}, u32[]{:S(2)}) collective-permute-start(bf16[128,768]{1,0:T(8,128)(2,1)S(1)} %get-tuple-element.24), channel_id=1, source_target_pairs={{0,16},{4,20},{8,24},{12,28},{16,0},{20,4},{24,8},{28,12},{1,17},{... | collective-permute-start | bytes 589832 | tf_op jit(solution)/shard_map/ppermute | solution.py:26
  46.5 12.6 %collective-permute-start.4 = (bf16[128,768]{1,0:T(8,128)(2,1)S(1)}, bf16[128,768]{1,0:T(8,128)(2,1)S(1)}, u32[]{:S(2)}, u32[]{:S(2)}) collective-permute-start(bf16[128,768]{1,0:T(8,128)(2,1)S(1)} %get-tuple-element.25), channel_id=1, source_target_pairs={{0,8},{4,12},{8,0},{12,4},{16,24},{20,28},{24,16},{28,20},{1,9},{5... | collective-permute-start | bytes 589832 | tf_op jit(solution)/shard_map/ppermute | solution.py:26
  48.0 15.4 %collective-permute-start.6 = (bf16[128,768]{1,0:T(8,128)(2,1)S(1)}, bf16[128,768]{1,0:T(8,128)(2,1)S(1)}, u32[]{:S(2)}, u32[]{:S(2)}) collective-permute-start(bf16[128,768]{1,0:T(8,128)(2,1)S(1)} %get-tuple-element.26), channel_id=1, source_target_pairs={{0,24},{4,28},{8,16},{12,20},{16,8},{20,12},{24,0},{28,4},{1,25},{... | collective-permute-start | bytes 589832 | tf_op jit(solution)/shard_map/ppermute | solution.py:26
  50.6 14.1 %collective-permute-start.5 = (bf16[128,768]{1,0:T(8,128)(2,1)S(1)}, bf16[128,768]{1,0:T(8,128)(2,1)S(1)}, u32[]{:S(2)}, u32[]{:S(2)}) collective-permute-start(bf16[128,768]{1,0:T(8,128)(2,1)S(1)} %get-tuple-element.27), channel_id=1, source_target_pairs={{0,16},{4,20},{8,24},{12,28},{16,0},{20,4},{24,8},{28,12},{1,17},{... | collective-permute-start | bytes 589832 | tf_op jit(solution)/shard_map/ppermute | solution.py:26
  66.8 12.9 %collective-permute-start.27 = (bf16[128,768]{1,0:T(8,128)(2,1)S(1)}, bf16[128,768]{1,0:T(8,128)(2,1)S(1)}, u32[]{:S(2)}, u32[]{:S(2)}) collective-permute-start(bf16[128,768]{1,0:T(8,128)(2,1)S(1)} %get-tuple-element.20.refs_0_), channel_id=1, source_target_pairs={{0,16},{4,20},{8,24},{12,28},{16,0},{20,4},{24,8},{28,12},{1,17},{... | collective-permute-start | bytes 589832 | tf_op jit(solution)/shard_map/ppermute | solution.py:26
  68.3 11.4 %collective-permute-start.12 = (bf16[128,768]{1,0:T(8,128)(2,1)S(1)}, bf16[128,768]{1,0:T(8,128)(2,1)S(1)}, u32[]{:S(2)}, u32[]{:S(2)}) collective-permute-start(bf16[128,768]{1,0:T(8,128)(2,1)S(1)} %get-tuple-element.21.refs_0_), channel_id=1, source_target_pairs={{0,24},{4,28},{8,16},{12,20},{16,8},{20,12},{24,0},{28,4},{1,25},{... | collective-permute-start | bytes 589832 | tf_op jit(solution)/shard_map/ppermute | solution.py:26
  68.8 14.7 %collective-permute-start.10 = (bf16[128,768]{1,0:T(8,128)(2,1)S(1)}, bf16[128,768]{1,0:T(8,128)(2,1)S(1)}, u32[]{:S(2)}, u32[]{:S(2)}) collective-permute-start(bf16[128,768]{1,0:T(8,128)(2,1)S(1)} %get-tuple-element.21.refs_0_), channel_id=1, source_target_pairs={{0,16},{4,20},{8,24},{12,28},{16,0},{20,4},{24,8},{28,12},{1,17},{... | collective-permute-start | bytes 589832 | tf_op jit(solution)/shard_map/ppermute | solution.py:26
  70.3 13.2 %collective-permute-start.8 = (bf16[128,768]{1,0:T(8,128)(2,1)S(1)}, bf16[128,768]{1,0:T(8,128)(2,1)S(1)}, u32[]{:S(2)}, u32[]{:S(2)}) collective-permute-start(bf16[128,768]{1,0:T(8,128)(2,1)S(1)} %get-tuple-element.21.refs_0_), channel_id=1, source_target_pairs={{0,8},{4,12},{8,0},{12,4},{16,24},{20,28},{24,16},{28,20},{1,9},{5... | collective-permute-start | bytes 589832 | tf_op jit(solution)/shard_map/ppermute | solution.py:26
  74.0 10.0 %collective-permute-start.25 = (bf16[128,768]{1,0:T(8,128)(2,1)S(1)}, bf16[128,768]{1,0:T(8,128)(2,1)S(1)}, u32[]{:S(2)}, u32[]{:S(2)}) collective-permute-start(bf16[128,768]{1,0:T(8,128)(2,1)S(1)} %get-tuple-element.20.refs_0_), channel_id=1, source_target_pairs={{0,8},{4,12},{8,0},{12,4},{16,24},{20,28},{24,16},{28,20},{1,9},{5... | collective-permute-start | bytes 589832 | tf_op jit(solution)/shard_map/ppermute | solution.py:26
  84.0 20.3 %collective-permute-start.24 = (bf16[128,768]{1,0:T(8,128)(2,1)S(1)}, bf16[128,768]{1,0:T(8,128)(2,1)S(1)}, u32[]{:S(2)}, u32[]{:S(2)}) collective-permute-start(bf16[128,768]{1,0:T(8,128)(2,1)S(1)} %get-tuple-element.20.refs_0_), channel_id=1, source_target_pairs={{0,4},{4,0},{8,12},{12,8},{16,20},{20,16},{24,28},{28,24},{1,5},{5... | collective-permute-start | bytes 589832 | tf_op jit(solution)/shard_map/ppermute | solution.py:26
  84.1 22.9 %collective-permute-start.30 = (bf16[128,768]{1,0:T(8,128)(2,1)S(1)}, bf16[128,768]{1,0:T(8,128)(2,1)S(1)}, u32[]{:S(2)}, u32[]{:S(2)}) collective-permute-start(bf16[128,768]{1,0:T(8,128)(2,1)S(1)} %collective-permute-done.29.refs_6_), channel_id=1, source_target_pairs={{0,4},{4,0},{8,12},{12,8},{16,20},{20,16},{24,28},{28,24},{1,5},{5... | collective-permute-start | bytes 589832 | tf_op jit(solution)/shard_map/ppermute | solution.py:26
  84.5 23.2 %collective-permute-start.28 = (bf16[128,768]{1,0:T(8,128)(2,1)S(1)}, bf16[128,768]{1,0:T(8,128)(2,1)S(1)}, u32[]{:S(2)}, u32[]{:S(2)}) collective-permute-start(bf16[128,768]{1,0:T(8,128)(2,1)S(1)} %collective-permute-done.27.refs_4_), channel_id=1, source_target_pairs={{0,4},{4,0},{8,12},{12,8},{16,20},{20,16},{24,28},{28,24},{1,5},{5... | collective-permute-start | bytes 589832 | tf_op jit(solution)/shard_map/ppermute | solution.py:26
  84.9 22.8 %collective-permute-start.26 = (bf16[128,768]{1,0:T(8,128)(2,1)S(1)}, bf16[128,768]{1,0:T(8,128)(2,1)S(1)}, u32[]{:S(2)}, u32[]{:S(2)}) collective-permute-start(bf16[128,768]{1,0:T(8,128)(2,1)S(1)} %collective-permute-done.25.refs_2_), channel_id=1, source_target_pairs={{0,4},{4,0},{8,12},{12,8},{16,20},{20,16},{24,28},{28,24},{1,5},{5... | collective-permute-start | bytes 589832 | tf_op jit(solution)/shard_map/ppermute | solution.py:26
  104.2 26.4 %collective-permute-start.17 = (bf16[32,1536]{1,0:T(8,128)(2,1)S(1)}, bf16[32,1536]{1,0:T(8,128)(2,1)S(1)}, u32[]{:S(2)}, u32[]{:S(2)}) collective-permute-start(bf16[32,1536]{1,0:T(8,128)(2,1)S(1)} %get-tuple-element.31), channel_id=1, source_target_pairs={{0,1},{1,0},{2,3},{3,2},{4,5},{5,4},{6,7},{7,6},{8,9},{9,8},{10,11... | collective-permute-start | bytes 294920 | tf_op jit(solution)/shard_map/ppermute | solution.py:26
  104.3 26.3 %collective-permute-start.19 = (bf16[32,1536]{1,0:T(8,128)(2,1)S(1)}, bf16[32,1536]{1,0:T(8,128)(2,1)S(1)}, u32[]{:S(2)}, u32[]{:S(2)}) collective-permute-start(bf16[32,1536]{1,0:T(8,128)(2,1)S(1)} %get-tuple-element.32), channel_id=1, source_target_pairs={{0,3},{1,2},{2,1},{3,0},{4,7},{5,6},{6,5},{7,4},{8,11},{9,10},{10,... | collective-permute-start | bytes 294920 | tf_op jit(solution)/shard_map/ppermute | solution.py:26
  107.0 23.6 %collective-permute-start.18 = (bf16[32,1536]{1,0:T(8,128)(2,1)S(1)}, bf16[32,1536]{1,0:T(8,128)(2,1)S(1)}, u32[]{:S(2)}, u32[]{:S(2)}) collective-permute-start(bf16[32,1536]{1,0:T(8,128)(2,1)S(1)} %get-tuple-element.33), channel_id=1, source_target_pairs={{0,2},{1,3},{2,0},{3,1},{4,6},{5,7},{6,4},{7,5},{8,10},{9,11},{10,... | collective-permute-start | bytes 294920 | tf_op jit(solution)/shard_map/ppermute | solution.py:26
  (13 other events, 132.3 us)

commit v2 on v1

--- a/solution.py
+++ b/solution.py
@@ -10,7 +10,7 @@
 BF16 = jnp.bfloat16
 F32 = jnp.float32
 MIB = 1024 * 1024
-VMEM_LIMIT = 48 * MIB
+VMEM_LIMIT = 14 * MIB
 
 
 def gelu_fn(value):
@@ -36,61 +36,61 @@
     return pl.BlockSpec(memory_space=pltpu.VMEM)
 
 
-def project_kernel(count, right_dim, me_ref, *refs):
-    pieces, (w_ref, keep_ref, send_ref, left) = refs[:count], refs[count:]
-    step = pl.program_id(0)
-
-    @pl.when(step == 0)
-    def _():
-        size = pieces[0].shape[0]
-        for i, piece in enumerate(pieces):
-            left[i * size : (i + 1) * size, :] = piece[...]
-
-    out = dot(left[...], w_ref[...], 1, right_dim).astype(BF16)
-
-    @pl.when(step % 2 == 0)
-    def _():
-        keep_ref[0] = out
-
-    @pl.when(step % 2 == 1)
-    def _():
-        send_ref[0] = out
+def project_kernel(count, by_rows, me_ref, *refs):
+    pieces, (source, held, keep_ref, send_ref, left, arrived) = refs[:count], refs[count:]
+    me = me_ref[0]
+    half, _, block = keep_ref.shape
+    size = pieces[0].shape[0]
+
+    def part(ref, r):
+        at = pl.ds(pl.multiple_of((me ^ r) * block, 128), block)
+        return ref.at[at, :] if by_rows else ref.at[:, at]
+
+    def load(r):
+        return pltpu.make_async_copy(part(source, r), part(held, r), arrived.at[r])
+
+    for r in range(2 * half):
+        load(r).start()
+    for i, piece in enumerate(pieces):
+        left[i * size : (i + 1) * size, :] = piece[...]
+
+    def step(i, unused):
+        for odd, out_ref in ((0, keep_ref), (1, send_ref)):
+            r = 2 * i + odd
+            load(r).wait()
+            weight = part(held, r)[...]
+            out_ref[i] = dot(left[...], weight, 1, 1 if by_rows else 0).astype(BF16)
+
+    lax.fori_loop(0, half, step, None)
 
 
 def project(me, pieces, weight, rows, by_rows):
     tokens = len(pieces) * pieces[0].shape[0]
     width = pieces[0].shape[1]
     hidden = weight.shape[0 if by_rows else 1]
-    block = hidden // rows
-    if by_rows:
-        w_spec = pl.BlockSpec((block, width), lambda s, me: (me[0] ^ s, 0))
-    else:
-        w_spec = pl.BlockSpec((width, block), lambda s, me: (0, me[0] ^ s))
-    out = jax.ShapeDtypeStruct((rows // 2, tokens, block), BF16)
-    out_spec = pl.BlockSpec((1, tokens, block), lambda s, me: (s // 2, 0, 0))
+    out = jax.ShapeDtypeStruct((rows // 2, tokens, hidden // rows), BF16)
     return pl.pallas_call(
-        functools.partial(project_kernel, len(pieces), 1 if by_rows else 0),
-        grid_spec=pltpu.PrefetchScalarGridSpec(
-            num_scalar_prefetch=1,
-            grid=(rows,),
-            in_specs=[whole()] * len(pieces) + [w_spec],
-            out_specs=[out_spec, out_spec],
-            scratch_shapes=[pltpu.VMEM((tokens, width), BF16)],
-        ),
-        out_shape=[out, out],
+        functools.partial(project_kernel, len(pieces), by_rows),
+        in_specs=[pl.BlockSpec(memory_space=pltpu.SMEM)]
+        + [whole()] * len(pieces)
+        + [pl.BlockSpec(memory_space=pl.ANY)],
+        out_specs=[whole()] * 3,
+        scratch_shapes=[pltpu.VMEM((tokens, width), BF16), pltpu.SemaphoreType.DMA((rows,))],
+        out_shape=[pltpu.VMEM(weight.shape, BF16), out, out],
         compiler_params=pltpu.CompilerParams(vmem_limit_bytes=VMEM_LIMIT),
         cost_estimate=pl.CostEstimate(
             flops=2 * tokens * width * hidden,
             bytes_accessed=2 * width * hidden + 2 * tokens * (width + hidden),
             transcendentals=0,
         ),
-    )(me, *pieces, weight)
+    )(me, *pieces, pltpu.with_memory_space_constraint(weight, pltpu.HBM))
 
 
 def back_kernel(rows, cols, by_rows, me_ref, *refs):
     blocks, refs = refs[:rows], refs[rows:]
     others, refs = refs[:cols], refs[cols:]
-    w_ref, out_ref, grad_ref, act, other, total = refs
+    w_ref, refs = refs[0], refs[1:]
+    outs, (grad_ref, act, other, total) = refs[:cols], refs[cols:]
     step = pl.program_id(0)
 
     @pl.when(step == 0)
@@ -103,7 +103,12 @@
         total[...] = jnp.zeros_like(total)
 
     value = act[step]
-    total[...] += dot(value, w_ref[...], 1, 0 if by_rows else 1)
+    block = value.shape[1]
+    at = pl.multiple_of((me_ref[0] ^ step) * block, 128)
+    if by_rows:
+        total[...] += dot(value, w_ref[pl.ds(at, block), :], 1, 0)
+    else:
+        total[...] += dot(value, w_ref[:, pl.ds(at, block)], 1, 1)
     if by_rows:
         grad_ref[...] = dot(value, other[...], 0, 0).astype(BF16)
     else:
@@ -112,8 +117,8 @@
     @pl.when(step == rows - 1)
     def _():
         size = others[0].shape[0]
-        for i in range(cols):
-            out_ref[i] = total[i * size : (i + 1) * size, :].astype(BF16)
+        for i, out_ref in enumerate(outs):
+            out_ref[...] = total[i * size : (i + 1) * size, :].astype(BF16)
 
 
 def back(me, blocks, others, weight, by_rows):
@@ -130,25 +135,23 @@
         grid_spec=pltpu.PrefetchScalarGridSpec(
             num_scalar_prefetch=1,
             grid=(rows,),
-            in_specs=[whole()] * (rows + cols) + [w_spec],
-            out_specs=[whole(), w_spec],
+            in_specs=[whole()] * (rows + cols + 1),
+            out_specs=[whole()] * cols + [w_spec],
             scratch_shapes=[
                 pltpu.VMEM((rows, tokens, block), BF16),
                 pltpu.VMEM((tokens, width), BF16),
                 pltpu.VMEM((tokens, width), F32),
             ],
         ),
-        out_shape=[
-            jax.ShapeDtypeStruct((cols, size, width), BF16),
-            jax.ShapeDtypeStruct(weight.shape, BF16),
-        ],
+        out_shape=[jax.ShapeDtypeStruct((size, width), BF16)] * cols
+        + [jax.ShapeDtypeStruct(weight.shape, BF16)],
         compiler_params=pltpu.CompilerParams(vmem_limit_bytes=VMEM_LIMIT),
         cost_estimate=pl.CostEstimate(
             flops=4 * tokens * width * hidden,
             bytes_accessed=4 * width * hidden + 2 * tokens * (2 * width + hidden),
             transcendentals=0,
         ),
-    )(me, *blocks, *others, weight)
+    )(me, *blocks, *others, pltpu.with_memory_space_constraint(weight, pltpu.VMEM))
 
 
 def gather_col(piece, cols):
@@ -183,12 +186,16 @@
     me = lax.axis_index("row").astype(jnp.int32).reshape(1)
     token_pieces = gather_col(tokens, cols)
     cot_pieces = gather_col(cotangent, cols)
-    hidden = scatter_row(*project(me, token_pieces, w_in, rows, False), rows)
-    grad_act = scatter_row(*project(me, cot_pieces, w_out, rows, True), rows)
-    act = gather_row(gelu_fn(hidden).astype(BF16), rows)
-    layer_parts, grad_w_out = back(me, act, cot_pieces, w_out, True)
+    w_in, *shares = project(me, token_pieces, w_in, rows, False)
+    hidden = scatter_row(*shares, rows)
+    w_out, *shares = project(me, cot_pieces, w_out, rows, True)
+    grad_act = scatter_row(*shares, rows)
+    act = gelu_fn(hidden).astype(BF16)
+    hidden, act = lax.optimization_barrier((hidden, act))
+    act = gather_row(act, rows)
+    *layer_parts, grad_w_out = back(me, act, cot_pieces, w_out, True)
     grad_hidden = gather_row(gelu_back(hidden, grad_act), rows)
-    token_parts, grad_w_in = back(me, grad_hidden, token_pieces, w_in, False)
+    *token_parts, grad_w_in = back(me, grad_hidden, token_pieces, w_in, False)
     layer_out = scatter_col(layer_parts, cols)
     grad_tokens = scatter_col(token_parts, cols)
     return (layer_out, grad_tokens, grad_w_in, grad_w_out)

time: 141 us -> 124 us (0.88)
  Pallas kernels: 59.7 us -> 43.1 us
  waiting for transfers between devices: 34.3 us -> 36.3 us
    pallas_call x2, Pallas kernels: 38 us -> 25.6 us  [back(): pl.pallas_call(functools.partial(back_kernel, rows, cols, by_rows), grid_...]
    pallas_call x2, Pallas kernels: 21.7 us -> 17.5 us  [project(): pl.pallas_call(functools.partial(project_kernel, len(pieces), by_rows), i...]
    ppermute x34, waiting for transfers between devices: 34.3 us -> 36.3 us  [swap(): return lax.ppermute(value, axis, [(i, i ^ flip) for i in range(count)])]
  transfers between devices with their start and end apart: 34 -> 34, of which waited for: 15 -> 13; matrix products, arithmetic and copies ran while one was open for 1% -> 1% of each run, Pallas kernels for 43% -> 35%
where the time goes in v2:
time: 124 us
  Pallas kernels  43.1 us (35%)
  starting transfers between devices  40.8 us (33%)
  waiting for transfers between devices  36.3 us (29%)
  other arithmetic  2.3 us (2%)
    ppermute x34, starting transfers between devices, swap(): return lax.ppermute(value, axis, [(i, i ^ flip) for i in range(count)])  40.8 us
    ppermute x34, waiting for transfers between devices, swap(): return lax.ppermute(value, axis, [(i, i ^ flip) for i in range(count)])  36.3 us
    pallas_call x2, Pallas kernels, back(): pl.pallas_call(functools.partial(back_kernel, rows, cols, by_rows), grid_...  25.6 us
    pallas_call x2, Pallas kernels, project(): pl.pallas_call(functools.partial(project_kernel, len(pieces), by_rows), i...  17.5 us
  transfers between devices with their start and end apart: 34, of which 13 were waited for; matrix products, arithmetic and copies ran while one was open for 1% of the time, Pallas kernels for 35%

profile of v2, /device:TPU:0, one launch (start us, length us, event | category | flops | bytes accessed | tf_op | source)
XLA Modules:
  0.0 124.1 jit_solution(9300118194753560638)
XLA Ops:
  0.6 5.1 %collective-permute-start.2 = (bf16[32,1536]{1,0:T(8,128)(2,1)}, bf16[32,1536]{1,0:T(8,128)(2,1)S(1)}, u32[]{:S(2)}, u32[]{:S(2)}) collective-permute-start(bf16[32,1536]{1,0:T(8,128)(2,1)} %refs_8_.3), channel_id=1, source_target_pairs={{0,3},{1,2},{2,1},{3,0},{4,7},{5,6},{6,5},{7,4},{8,11},{9,10},{10,... | collective-permute-start | bytes 294920 | tf_op jit(solution)/shard_map/ppermute | solution.py:26
  6.4 3.7 %collective-permute-start.16 = (bf16[32,1536]{1,0:T(8,128)(2,1)}, bf16[32,1536]{1,0:T(8,128)(2,1)S(1)}, u32[]{:S(2)}, u32[]{:S(2)}) collective-permute-start(bf16[32,1536]{1,0:T(8,128)(2,1)} %refs_8_.2), channel_id=1, source_target_pairs={{0,3},{1,2},{2,1},{3,0},{4,7},{5,6},{6,5},{7,4},{8,11},{9,10},{10,... | collective-permute-start | bytes 294920 | tf_op jit(solution)/shard_map/ppermute | solution.py:26
  10.1 6.7 %collective-permute-start.14 = (bf16[32,1536]{1,0:T(8,128)(2,1)}, bf16[32,1536]{1,0:T(8,128)(2,1)S(1)}, u32[]{:S(2)}, u32[]{:S(2)}) collective-permute-start(bf16[32,1536]{1,0:T(8,128)(2,1)} %refs_8_.2), channel_id=1, source_target_pairs={{0,1},{1,0},{2,3},{3,2},{4,5},{5,4},{6,7},{7,6},{8,9},{9,8},{10,11... | collective-permute-start | bytes 294920 | tf_op jit(solution)/shard_map/ppermute | solution.py:26
  16.9 2.5 %collective-permute-done.1.refs_2_.refs_10_ = bf16[32,1536]{1,0:T(8,128)(2,1)S(1)} collective-permute-done((bf16[32,1536]{1,0:T(8,128)(2,1)}, bf16[32,1536]{1,0:T(8,128)(2,1)S(1)}, u32[]{:S(2)}, u32[]{:S(2)}) %collective-permute-start.1) | collective-permute-done | bytes 98336 | tf_op jit(solution)/shard_map/ppermute | solution.py:26
  20.3 7.2 %shard_map.75 = (bf16[1536,6144]{1,0:T(8,128)(2,1)S(1)}, bf16[4,128,768]{2,1,0:T(8,128)(2,1)S(1)}, bf16[4,128,768]{2,1,0:T(8,128)(2,1)S(1)}) custom-call(s32[1]{0:T(128)} %bitcast.me_ref, bf16[32,1536]{1,0:T(8,128)(2,1)S(1)} %copy-done, bf16[32,1536]{1,0:T(8,128)(2,1)S(1)} %collective-permute-done.refs_1_.refs_9_, ...), custom_call_target="tpu_custom_call" | custom-call | flops 2415919104 | bytes 20840448 | tf_op jit(solution)/shard_map/pallas_call | solution.py:72
  27.7 10.3 %shard_map.76 = (bf16[6144,1536]{1,0:T(8,128)(2,1)S(1)}, bf16[4,128,768]{2,1,0:T(8,128)(2,1)S(1)}, bf16[4,128,768]{2,1,0:T(8,128)(2,1)S(1)}) custom-call(s32[1]{0:T(128)} %bitcast.me_ref, bf16[32,1536]{1,0:T(8,128)(2,1)S(1)} %copy-done.2, bf16[32,1536]{1,0:T(8,128)(2,1)S(1)} %collective-permute-done.14.refs_1_.refs_9_, ...), custom_call_target="tpu_custom_call" | custom-call | flops 2415919104 | bytes 20840448 | tf_op jit(solution)/shard_map/pallas_call | solution.py:72
  38.6 1.6 %collective-permute-start.4 = (bf16[128,768]{1,0:T(8,128)(2,1)S(1)}, bf16[128,768]{1,0:T(8,128)(2,1)S(1)}, u32[]{:S(2)}, u32[]{:S(2)}) collective-permute-start(bf16[128,768]{1,0:T(8,128)(2,1)S(1)} %get-tuple-element.45), channel_id=1, source_target_pairs={{0,8},{4,12},{8,0},{12,4},{16,24},{20,28},{24,16},{28,20},{1,9},{5... | collective-permute-start | bytes 589832 | tf_op jit(solution)/shard_map/ppermute | solution.py:26
  40.2 1.5 %collective-permute-start.6 = (bf16[128,768]{1,0:T(8,128)(2,1)S(1)}, bf16[128,768]{1,0:T(8,128)(2,1)S(1)}, u32[]{:S(2)}, u32[]{:S(2)}) collective-permute-start(bf16[128,768]{1,0:T(8,128)(2,1)S(1)} %get-tuple-element.46), channel_id=1, source_target_pairs={{0,24},{4,28},{8,16},{12,20},{16,8},{20,12},{24,0},{28,4},{1,25},{... | collective-permute-start | bytes 589832 | tf_op jit(solution)/shard_map/ppermute | solution.py:26
  42.3 1.6 %collective-permute-start.21 = (bf16[128,768]{1,0:T(8,128)(2,1)S(1)}, bf16[128,768]{1,0:T(8,128)(2,1)S(1)}, u32[]{:S(2)}, u32[]{:S(2)}) collective-permute-start(bf16[128,768]{1,0:T(8,128)(2,1)S(1)} %get-tuple-element.42), channel_id=1, source_target_pairs={{0,8},{4,12},{8,0},{12,4},{16,24},{20,28},{24,16},{28,20},{1,9},{5... | collective-permute-start | bytes 589832 | tf_op jit(solution)/shard_map/ppermute | solution.py:26
  46.5 1.5 %collective-permute-start.22 = (bf16[128,768]{1,0:T(8,128)(2,1)S(1)}, bf16[128,768]{1,0:T(8,128)(2,1)S(1)}, u32[]{:S(2)}, u32[]{:S(2)}) collective-permute-start(bf16[128,768]{1,0:T(8,128)(2,1)S(1)} %get-tuple-element.44), channel_id=1, source_target_pairs={{0,16},{4,20},{8,24},{12,28},{16,0},{20,4},{24,8},{28,12},{1,17},{... | collective-permute-start | bytes 589832 | tf_op jit(solution)/shard_map/ppermute | solution.py:26
  48.0 3.7 %collective-permute-done.6 = bf16[128,768]{1,0:T(8,128)(2,1)S(1)} collective-permute-done((bf16[128,768]{1,0:T(8,128)(2,1)S(1)}, bf16[128,768]{1,0:T(8,128)(2,1)S(1)}, u32[]{:S(2)}, u32[]{:S(2)}) %collective-permute-start.6) | collective-permute-done | bytes 196640 | tf_op jit(solution)/shard_map/ppermute | solution.py:26
  51.7 2.0 %collective-permute-done.5 = bf16[128,768]{1,0:T(8,128)(2,1)S(1)} collective-permute-done((bf16[128,768]{1,0:T(8,128)(2,1)S(1)}, bf16[128,768]{1,0:T(8,128)(2,1)S(1)}, u32[]{:S(2)}, u32[]{:S(2)}) %collective-permute-start.5) | collective-permute-done | bytes 196640 | tf_op jit(solution)/shard_map/ppermute | solution.py:26
  54.9 4.4 %collective-permute-done.23 = bf16[128,768]{1,0:T(8,128)(2,1)S(1)} collective-permute-done((bf16[128,768]{1,0:T(8,128)(2,1)S(1)}, bf16[128,768]{1,0:T(8,128)(2,1)S(1)}, u32[]{:S(2)}, u32[]{:S(2)}) %collective-permute-start.23) | collective-permute-done | bytes 196640 | tf_op jit(solution)/shard_map/ppermute | solution.py:26
  61.0 1.5 %collective-permute-start.29 = (bf16[128,768]{1,0:T(8,128)(2,1)S(1)}, bf16[128,768]{1,0:T(8,128)(2,1)S(1)}, u32[]{:S(2)}, u32[]{:S(2)}) collective-permute-start(bf16[128,768]{1,0:T(8,128)(2,1)S(1)} %fusion.6.refs_0_), channel_id=1, source_target_pairs={{0,24},{4,28},{8,16},{12,20},{16,8},{20,12},{24,0},{28,4},{1,25},{... | collective-permute-start | bytes 589832 | tf_op jit(solution)/shard_map/ppermute | solution.py:26
  62.5 1.5 %collective-permute-start.27 = (bf16[128,768]{1,0:T(8,128)(2,1)S(1)}, bf16[128,768]{1,0:T(8,128)(2,1)S(1)}, u32[]{:S(2)}, u32[]{:S(2)}) collective-permute-start(bf16[128,768]{1,0:T(8,128)(2,1)S(1)} %fusion.6.refs_0_), channel_id=1, source_target_pairs={{0,16},{4,20},{8,24},{12,28},{16,0},{20,4},{24,8},{28,12},{1,17},{... | collective-permute-start | bytes 589832 | tf_op jit(solution)/shard_map/ppermute | solution.py:26
  66.0 3.5 %collective-permute-done.29.refs_6_ = bf16[128,768]{1,0:T(8,128)(2,1)S(1)} collective-permute-done((bf16[128,768]{1,0:T(8,128)(2,1)S(1)}, bf16[128,768]{1,0:T(8,128)(2,1)S(1)}, u32[]{:S(2)}, u32[]{:S(2)}) %collective-permute-start.29) | collective-permute-done | bytes 196640 | tf_op jit(solution)/shard_map/ppermute | solution.py:26
  70.3 6.1 %collective-permute-done.27.refs_4_ = bf16[128,768]{1,0:T(8,128)(2,1)S(1)} collective-permute-done((bf16[128,768]{1,0:T(8,128)(2,1)S(1)}, bf16[128,768]{1,0:T(8,128)(2,1)S(1)}, u32[]{:S(2)}, u32[]{:S(2)}) %collective-permute-start.27) | collective-permute-done | bytes 196640 | tf_op jit(solution)/shard_map/ppermute | solution.py:26
  77.0 2.2 %collective-permute-done.10.refs_4_ = bf16[128,768]{1,0:T(8,128)(2,1)S(1)} collective-permute-done((bf16[128,768]{1,0:T(8,128)(2,1)S(1)}, bf16[128,768]{1,0:T(8,128)(2,1)S(1)}, u32[]{:S(2)}, u32[]{:S(2)}) %collective-permute-start.10) | collective-permute-done | bytes 196640 | tf_op jit(solution)/shard_map/ppermute | solution.py:26
  79.2 2.8 %collective-permute-done.8.refs_2_ = bf16[128,768]{1,0:T(8,128)(2,1)S(1)} collective-permute-done((bf16[128,768]{1,0:T(8,128)(2,1)S(1)}, bf16[128,768]{1,0:T(8,128)(2,1)S(1)}, u32[]{:S(2)}, u32[]{:S(2)}) %collective-permute-start.8) | collective-permute-done | bytes 196640 | tf_op jit(solution)/shard_map/ppermute | solution.py:26
  82.6 14.2 %shard_map.78 = (bf16[32,1536]{1,0:T(8,128)(2,1)S(1)}, bf16[32,1536]{1,0:T(8,128)(2,1)S(1)}, bf16[32,1536]{1,0:T(8,128)(2,1)S(1)}, bf16[32,1536]{1,0:T(8,128)(2,1)S(1)}, bf16[1536,6144]{1,0:T(8,128)(2,1)}) custom-call(s32[1]{0:T(128)} %bitcast.me_ref, bf16[128,768]{1,0:T(8,128)(2,1)S(1)} %fusion.6.refs_0_, ...), custom_call_target="tpu_custom_call" | custom-call | flops 4831838208 | bytes 40108032 | tf_op jit(solution)/shard_map/pallas_call | solution.py:133
  96.9 3.2 %collective-permute-start.32 = (bf16[32,1536]{1,0:T(8,128)(2,1)S(1)}, bf16[32,1536]{1,0:T(8,128)(2,1)S(1)}, u32[]{:S(2)}, u32[]{:S(2)}) collective-permute-start(bf16[32,1536]{1,0:T(8,128)(2,1)S(1)} %get-tuple-element.36), channel_id=1, source_target_pairs={{0,2},{1,3},{2,0},{3,1},{4,6},{5,7},{6,4},{7,5},{8,10},{9,11},{10,... | collective-permute-start | bytes 294920 | tf_op jit(solution)/shard_map/ppermute | solution.py:26
  101.3 11.4 %shard_map.77 = (bf16[32,1536]{1,0:T(8,128)(2,1)S(1)}, bf16[32,1536]{1,0:T(8,128)(2,1)S(1)}, bf16[32,1536]{1,0:T(8,128)(2,1)S(1)}, bf16[32,1536]{1,0:T(8,128)(2,1)S(1)}, bf16[6144,1536]{1,0:T(8,128)(2,1)}) custom-call(s32[1]{0:T(128)} %bitcast.me_ref, bf16[128,768]{1,0:T(8,128)(2,1)S(1)} %get-tuple-element.24.refs_0_, ...), custom_call_target="tpu_custom_call" | custom-call | flops 4831838208 | bytes 40108032 | tf_op jit(solution)/shard_map/pallas_call | solution.py:133
  112.7 3.2 %collective-permute-start.18 = (bf16[32,1536]{1,0:T(8,128)(2,1)S(1)}, bf16[32,1536]{1,0:T(8,128)(2,1)S(1)}, u32[]{:S(2)}, u32[]{:S(2)}) collective-permute-start(bf16[32,1536]{1,0:T(8,128)(2,1)S(1)} %get-tuple-element.28), channel_id=1, source_target_pairs={{0,2},{1,3},{2,0},{3,1},{4,6},{5,7},{6,4},{7,5},{8,10},{9,11},{10,... | collective-permute-start | bytes 294920 | tf_op jit(solution)/shard_map/ppermute | solution.py:26
  118.4 5.1 %collective-permute-done.18 = bf16[32,1536]{1,0:T(8,128)(2,1)S(1)} collective-permute-done((bf16[32,1536]{1,0:T(8,128)(2,1)S(1)}, bf16[32,1536]{1,0:T(8,128)(2,1)S(1)}, u32[]{:S(2)}, u32[]{:S(2)}) %collective-permute-start.18) | collective-permute-done | bytes 98336 | tf_op jit(solution)/shard_map/ppermute | solution.py:26
  (60 shorter events, 16.9 us)
Async XLA Ops:
  5.7 13.6 %collective-permute-start.1 = (bf16[32,1536]{1,0:T(8,128)(2,1)}, bf16[32,1536]{1,0:T(8,128)(2,1)S(1)}, u32[]{:S(2)}, u32[]{:S(2)}) collective-permute-start(bf16[32,1536]{1,0:T(8,128)(2,1)} %refs_8_.3), channel_id=1, source_target_pairs={{0,2},{1,3},{2,0},{3,1},{4,6},{5,7},{6,4},{7,5},{8,10},{9,11},{10,... | collective-permute-start | bytes 294920 | tf_op jit(solution)/shard_map/ppermute | solution.py:26
  5.7 13.6 %collective-permute-start = (bf16[32,1536]{1,0:T(8,128)(2,1)}, bf16[32,1536]{1,0:T(8,128)(2,1)S(1)}, u32[]{:S(2)}, u32[]{:S(2)}) collective-permute-start(bf16[32,1536]{1,0:T(8,128)(2,1)} %refs_8_.3), channel_id=1, source_target_pairs={{0,1},{1,0},{2,3},{3,2},{4,5},{5,4},{6,7},{7,6},{8,9},{9,8},{10,11... | collective-permute-start | bytes 294920 | tf_op jit(solution)/shard_map/ppermute | solution.py:26
  6.4 21.2 %collective-permute-start.16 = (bf16[32,1536]{1,0:T(8,128)(2,1)}, bf16[32,1536]{1,0:T(8,128)(2,1)S(1)}, u32[]{:S(2)}, u32[]{:S(2)}) collective-permute-start(bf16[32,1536]{1,0:T(8,128)(2,1)} %refs_8_.2), channel_id=1, source_target_pairs={{0,3},{1,2},{2,1},{3,0},{4,7},{5,6},{6,5},{7,4},{8,11},{9,10},{10,... | collective-permute-start | bytes 294920 | tf_op jit(solution)/shard_map/ppermute | solution.py:26
  10.1 17.5 %collective-permute-start.15 = (bf16[32,1536]{1,0:T(8,128)(2,1)}, bf16[32,1536]{1,0:T(8,128)(2,1)S(1)}, u32[]{:S(2)}, u32[]{:S(2)}) collective-permute-start(bf16[32,1536]{1,0:T(8,128)(2,1)} %refs_8_.2), channel_id=1, source_target_pairs={{0,2},{1,3},{2,0},{3,1},{4,6},{5,7},{6,4},{7,5},{8,10},{9,11},{10,... | collective-permute-start | bytes 294920 | tf_op jit(solution)/shard_map/ppermute | solution.py:26
  10.1 17.5 %collective-permute-start.14 = (bf16[32,1536]{1,0:T(8,128)(2,1)}, bf16[32,1536]{1,0:T(8,128)(2,1)S(1)}, u32[]{:S(2)}, u32[]{:S(2)}) collective-permute-start(bf16[32,1536]{1,0:T(8,128)(2,1)} %refs_8_.2), channel_id=1, source_target_pairs={{0,1},{1,0},{2,3},{3,2},{4,5},{5,4},{6,7},{7,6},{8,9},{9,8},{10,11... | collective-permute-start | bytes 294920 | tf_op jit(solution)/shard_map/ppermute | solution.py:26
  27.5 11.0 %collective-permute-start.3 = (bf16[4,128,768]{2,1,0:T(8,128)(2,1)S(1)}, bf16[4,128,768]{2,1,0:T(8,128)(2,1)S(1)}, u32[]{:S(2)}, u32[]{:S(2)}) collective-permute-start(bf16[4,128,768]{2,1,0:T(8,128)(2,1)S(1)} %get-tuple-element.23), channel_id=1, source_target_pairs={{0,4},{4,0},{8,12},{12,8},{16,20},{20,16},{24,28},{28,24},{1,5},{5... | collective-permute-start | bytes 2359304 | tf_op jit(solution)/shard_map/ppermute | solution.py:26
  40.2 11.5 %collective-permute-start.6 = (bf16[128,768]{1,0:T(8,128)(2,1)S(1)}, bf16[128,768]{1,0:T(8,128)(2,1)S(1)}, u32[]{:S(2)}, u32[]{:S(2)}) collective-permute-start(bf16[128,768]{1,0:T(8,128)(2,1)S(1)} %get-tuple-element.46), channel_id=1, source_target_pairs={{0,24},{4,28},{8,16},{12,20},{16,8},{20,12},{24,0},{28,4},{1,25},{... | collective-permute-start | bytes 589832 | tf_op jit(solution)/shard_map/ppermute | solution.py:26
  41.7 12.0 %collective-permute-start.5 = (bf16[128,768]{1,0:T(8,128)(2,1)S(1)}, bf16[128,768]{1,0:T(8,128)(2,1)S(1)}, u32[]{:S(2)}, u32[]{:S(2)}) collective-permute-start(bf16[128,768]{1,0:T(8,128)(2,1)S(1)} %get-tuple-element.47), channel_id=1, source_target_pairs={{0,16},{4,20},{8,24},{12,28},{16,0},{20,4},{24,8},{28,12},{1,17},{... | collective-permute-start | bytes 589832 | tf_op jit(solution)/shard_map/ppermute | solution.py:26
  42.3 12.6 %collective-permute-start.21 = (bf16[128,768]{1,0:T(8,128)(2,1)S(1)}, bf16[128,768]{1,0:T(8,128)(2,1)S(1)}, u32[]{:S(2)}, u32[]{:S(2)}) collective-permute-start(bf16[128,768]{1,0:T(8,128)(2,1)S(1)} %get-tuple-element.42), channel_id=1, source_target_pairs={{0,8},{4,12},{8,0},{12,4},{16,24},{20,28},{24,16},{28,20},{1,9},{5... | collective-permute-start | bytes 589832 | tf_op jit(solution)/shard_map/ppermute | solution.py:26
  43.9 15.4 %collective-permute-start.23 = (bf16[128,768]{1,0:T(8,128)(2,1)S(1)}, bf16[128,768]{1,0:T(8,128)(2,1)S(1)}, u32[]{:S(2)}, u32[]{:S(2)}) collective-permute-start(bf16[128,768]{1,0:T(8,128)(2,1)S(1)} %get-tuple-element.43), channel_id=1, source_target_pairs={{0,24},{4,28},{8,16},{12,20},{16,8},{20,12},{24,0},{28,4},{1,25},{... | collective-permute-start | bytes 589832 | tf_op jit(solution)/shard_map/ppermute | solution.py:26
  46.5 14.1 %collective-permute-start.22 = (bf16[128,768]{1,0:T(8,128)(2,1)S(1)}, bf16[128,768]{1,0:T(8,128)(2,1)S(1)}, u32[]{:S(2)}, u32[]{:S(2)}) collective-permute-start(bf16[128,768]{1,0:T(8,128)(2,1)S(1)} %get-tuple-element.44), channel_id=1, source_target_pairs={{0,16},{4,20},{8,24},{12,28},{16,0},{20,4},{24,8},{28,12},{1,17},{... | collective-permute-start | bytes 589832 | tf_op jit(solution)/shard_map/ppermute | solution.py:26
  62.5 13.9 %collective-permute-start.27 = (bf16[128,768]{1,0:T(8,128)(2,1)S(1)}, bf16[128,768]{1,0:T(8,128)(2,1)S(1)}, u32[]{:S(2)}, u32[]{:S(2)}) collective-permute-start(bf16[128,768]{1,0:T(8,128)(2,1)S(1)} %fusion.6.refs_0_), channel_id=1, source_target_pairs={{0,16},{4,20},{8,24},{12,28},{16,0},{20,4},{24,8},{28,12},{1,17},{... | collective-permute-start | bytes 589832 | tf_op jit(solution)/shard_map/ppermute | solution.py:26
  64.0 12.4 %collective-permute-start.25 = (bf16[128,768]{1,0:T(8,128)(2,1)S(1)}, bf16[128,768]{1,0:T(8,128)(2,1)S(1)}, u32[]{:S(2)}, u32[]{:S(2)}) collective-permute-start(bf16[128,768]{1,0:T(8,128)(2,1)S(1)} %fusion.6.refs_0_), channel_id=1, source_target_pairs={{0,8},{4,12},{8,0},{12,4},{16,24},{20,28},{24,16},{28,20},{1,9},{5... | collective-permute-start | bytes 589832 | tf_op jit(solution)/shard_map/ppermute | solution.py:26
  64.6 11.8 %collective-permute-start.24 = (bf16[128,768]{1,0:T(8,128)(2,1)S(1)}, bf16[128,768]{1,0:T(8,128)(2,1)S(1)}, u32[]{:S(2)}, u32[]{:S(2)}) collective-permute-start(bf16[128,768]{1,0:T(8,128)(2,1)S(1)} %fusion.6.refs_0_), channel_id=1, source_target_pairs={{0,4},{4,0},{8,12},{12,8},{16,20},{20,16},{24,28},{28,24},{1,5},{5... | collective-permute-start | bytes 589832 | tf_op jit(solution)/shard_map/ppermute | solution.py:26
  64.6 12.3 %collective-permute-start.12 = (bf16[128,768]{1,0:T(8,128)(2,1)S(1)}, bf16[128,768]{1,0:T(8,128)(2,1)S(1)}, u32[]{:S(2)}, u32[]{:S(2)}) collective-permute-start(bf16[128,768]{1,0:T(8,128)(2,1)S(1)} %get-tuple-element.24.refs_0_), channel_id=1, source_target_pairs={{0,24},{4,28},{8,16},{12,20},{16,8},{20,12},{24,0},{28,4},{1,25},{... | collective-permute-start | bytes 589832 | tf_op jit(solution)/shard_map/ppermute | solution.py:26
  69.5 9.8 %collective-permute-start.10 = (bf16[128,768]{1,0:T(8,128)(2,1)S(1)}, bf16[128,768]{1,0:T(8,128)(2,1)S(1)}, u32[]{:S(2)}, u32[]{:S(2)}) collective-permute-start(bf16[128,768]{1,0:T(8,128)(2,1)S(1)} %get-tuple-element.24.refs_0_), channel_id=1, source_target_pairs={{0,16},{4,20},{8,24},{12,28},{16,0},{20,4},{24,8},{28,12},{1,17},{... | collective-permute-start | bytes 589832 | tf_op jit(solution)/shard_map/ppermute | solution.py:26
  79.2 17.6 %collective-permute-start.7 = (bf16[128,768]{1,0:T(8,128)(2,1)S(1)}, bf16[128,768]{1,0:T(8,128)(2,1)S(1)}, u32[]{:S(2)}, u32[]{:S(2)}) collective-permute-start(bf16[128,768]{1,0:T(8,128)(2,1)S(1)} %get-tuple-element.24.refs_0_), channel_id=1, source_target_pairs={{0,4},{4,0},{8,12},{12,8},{16,20},{20,16},{24,28},{28,24},{1,5},{5... | collective-permute-start | bytes 589832 | tf_op jit(solution)/shard_map/ppermute | solution.py:26
  82.1 18.0 %collective-permute-start.13 = (bf16[128,768]{1,0:T(8,128)(2,1)S(1)}, bf16[128,768]{1,0:T(8,128)(2,1)S(1)}, u32[]{:S(2)}, u32[]{:S(2)}) collective-permute-start(bf16[128,768]{1,0:T(8,128)(2,1)S(1)} %collective-permute-done.12.refs_6_), channel_id=1, source_target_pairs={{0,4},{4,0},{8,12},{12,8},{16,20},{20,16},{24,28},{28,24},{1,5},{5... | collective-permute-start | bytes 589832 | tf_op jit(solution)/shard_map/ppermute | solution.py:26
  82.1 19.2 %collective-permute-start.11 = (bf16[128,768]{1,0:T(8,128)(2,1)S(1)}, bf16[128,768]{1,0:T(8,128)(2,1)S(1)}, u32[]{:S(2)}, u32[]{:S(2)}) collective-permute-start(bf16[128,768]{1,0:T(8,128)(2,1)S(1)} %collective-permute-done.10.refs_4_), channel_id=1, source_target_pairs={{0,4},{4,0},{8,12},{12,8},{16,20},{20,16},{24,28},{28,24},{1,5},{5... | collective-permute-start | bytes 589832 | tf_op jit(solution)/shard_map/ppermute | solution.py:26
  82.6 18.7 %collective-permute-start.9 = (bf16[128,768]{1,0:T(8,128)(2,1)S(1)}, bf16[128,768]{1,0:T(8,128)(2,1)S(1)}, u32[]{:S(2)}, u32[]{:S(2)}) collective-permute-start(bf16[128,768]{1,0:T(8,128)(2,1)S(1)} %collective-permute-done.8.refs_2_), channel_id=1, source_target_pairs={{0,4},{4,0},{8,12},{12,8},{16,20},{20,16},{24,28},{28,24},{1,5},{5... | collective-permute-start | bytes 589832 | tf_op jit(solution)/shard_map/ppermute | solution.py:26
  96.9 19.0 %collective-permute-start.31 = (bf16[32,1536]{1,0:T(8,128)(2,1)S(1)}, bf16[32,1536]{1,0:T(8,128)(2,1)S(1)}, u32[]{:S(2)}, u32[]{:S(2)}) collective-permute-start(bf16[32,1536]{1,0:T(8,128)(2,1)S(1)} %get-tuple-element.35), channel_id=1, source_target_pairs={{0,1},{1,0},{2,3},{3,2},{4,5},{5,4},{6,7},{7,6},{8,9},{9,8},{10,11... | collective-permute-start | bytes 294920 | tf_op jit(solution)/shard_map/ppermute | solution.py:26
  96.9 20.2 %collective-permute-start.32 = (bf16[32,1536]{1,0:T(8,128)(2,1)S(1)}, bf16[32,1536]{1,0:T(8,128)(2,1)S(1)}, u32[]{:S(2)}, u32[]{:S(2)}) collective-permute-start(bf16[32,1536]{1,0:T(8,128)(2,1)S(1)} %get-tuple-element.36), channel_id=1, source_target_pairs={{0,2},{1,3},{2,0},{3,1},{4,6},{5,7},{6,4},{7,5},{8,10},{9,11},{10,... | collective-permute-start | bytes 294920 | tf_op jit(solution)/shard_map/ppermute | solution.py:26
  100.1 17.0 %collective-permute-start.33 = (bf16[32,1536]{1,0:T(8,128)(2,1)S(1)}, bf16[32,1536]{1,0:T(8,128)(2,1)S(1)}, u32[]{:S(2)}, u32[]{:S(2)}) collective-permute-start(bf16[32,1536]{1,0:T(8,128)(2,1)S(1)} %get-tuple-element.37), channel_id=1, source_target_pairs={{0,3},{1,2},{2,1},{3,0},{4,7},{5,6},{6,5},{7,4},{8,11},{9,10},{10,... | collective-permute-start | bytes 294920 | tf_op jit(solution)/shard_map/ppermute | solution.py:26
  112.7 10.7 %collective-permute-start.18 = (bf16[32,1536]{1,0:T(8,128)(2,1)S(1)}, bf16[32,1536]{1,0:T(8,128)(2,1)S(1)}, u32[]{:S(2)}, u32[]{:S(2)}) collective-permute-start(bf16[32,1536]{1,0:T(8,128)(2,1)S(1)} %get-tuple-element.28), channel_id=1, source_target_pairs={{0,2},{1,3},{2,0},{3,1},{4,6},{5,7},{6,4},{7,5},{8,10},{9,11},{10,... | collective-permute-start | bytes 294920 | tf_op jit(solution)/shard_map/ppermute | solution.py:26
  (13 other events, 137.1 us)

commit v3 on v0

v3 whole, which is shorter than its diff:
```python
import functools

import jax
import jax.numpy as jnp
from jax import lax
from jax.experimental import pallas as pl
from jax.experimental.pallas import tpu as pltpu
from jax.sharding import PartitionSpec as P

BF16 = jnp.bfloat16
F32 = jnp.float32
VMEM_LIMIT = 10 * 1024 * 1024
WRITES = 6


def gelu_fn(value):
    return jax.nn.gelu(value, approximate=True)


def gelu_back(hidden, grad_act):
    unused, pullback = jax.vjp(gelu_fn, hidden)
    return pullback(grad_act)[0].astype(BF16)


def swap(value, axis, flip, count):
    return lax.ppermute(value, axis, [(i, i ^ flip) for i in range(count)])


def dot(left, right, left_dim, right_dim):
    return lax.dot_general(
        left, right, (((left_dim,), (right_dim,)), ((), ())), preferred_element_type=F32
    )


def call(kernel, arrays, outs, flops, moved, after=(), scratch=()):
    spaces = {"smem": pltpu.SMEM, "vmem": pltpu.VMEM, "hbm": pl.ANY}
    operands = []
    for space, value in arrays:
        if space != "smem":
            value = pltpu.with_memory_space_constraint(
                value, pltpu.HBM if space == "hbm" else pltpu.VMEM
            )
        operands.append(value)
    return pl.pallas_call(
        kernel,
        in_specs=[pl.BlockSpec(memory_space=spaces[space]) for space, value in arrays]
        + [pl.BlockSpec(memory_space=pl.ANY)] * len(after),
        out_specs=[pl.BlockSpec(memory_space=spaces[space]) for space, value in outs],
        scratch_shapes=list(scratch),
        out_shape=[
            pltpu.VMEM(shape, dtype) if space == "vmem" else jax.ShapeDtypeStruct(shape, dtype)
            for space, (shape, dtype) in outs
        ],
        compiler_params=pltpu.CompilerParams(vmem_limit_bytes=VMEM_LIMIT),
        cost_estimate=pl.CostEstimate(flops=flops, bytes_accessed=moved, transcendentals=0),
    )(*operands, *after)


def in_vmem(values):
    return [("vmem", value) for value in values]


def join(pieces, out):
    at = 0
    for piece in pieces:
        out[at : at + piece.shape[0], :] = piece[...]
        at += piece.shape[0]


def place(pieces, order, out):
    size, order = pieces[0].shape[0], list(order)
    for piece in pieces:
        for at in range(0, piece.shape[0], size):
            to = order.pop(0) * size
            out[to : to + size, :] = piece[at : at + size, :]


def joined(pieces, after=()):
    rows = sum(piece.shape[0] for piece in pieces)

    def kernel(*refs):
        join(refs[: len(pieces)], refs[-1])

    return call(
        kernel, in_vmem(pieces), [("vmem", ((rows, pieces[0].shape[1]), BF16))], 0, 0, after
    )[0]


class Weight:
    def __init__(self, me, value, rows, by_rows):
        self.me, self.value, self.by_rows = me, value, by_rows
        self.block = value.shape[0 if by_rows else 1] // rows
        self.width = value.shape[1 if by_rows else 0]
        self.held = {}

    def shape(self):
        return ((2, self.block, self.width) if self.by_rows else (2, self.width, self.block), BF16)

    def part(self, ref, me, r):
        at = pl.ds(pl.multiple_of((me ^ r) * self.block, 128), self.block)
        return ref.at[at, :] if self.by_rows else ref.at[:, at]

    def copies(self, source, helds, arrived, me, chips):
        return [
            pltpu.make_async_copy(
                self.part(source, me, 2 * chip + odd), held.at[odd], arrived.at[2 * i + odd]
            )
            for i, (chip, held) in enumerate(zip(chips, helds))
            for odd in range(2)
        ]

    def moved(self, chips):
        return 4 * len(chips) * self.block * self.width


def load(weight, chips, after=()):
    def kernel(me_ref, source, *refs):
        refs = refs[len(after) :]
        copies = weight.copies(source, refs[:-1], refs[-1], me_ref[0], chips)
        for copy in copies:
            copy.start()
        for copy in copies:
            copy.wait()

    helds = call(
        kernel,
        [("smem", weight.me), ("hbm", weight.value)],
        [("vmem", weight.shape())] * len(chips),
        0,
        0,
        after,
        [pltpu.SemaphoreType.DMA((2 * len(chips),))],
    )
    weight.held.update(zip(chips, helds))


def project(weight, shards, chips, after=(), coming=None, coming_chips=()):
    pieces, order = shards
    tokens, n = sum(piece.shape[0] for piece in pieces), len(chips)
    block, by_rows = weight.block, weight.by_rows
    more = len(coming_chips)

    def kernel(me_ref, *refs):
        piece_refs, refs = refs[: len(pieces)], refs[len(pieces) :]
        parts, refs = refs[:n], refs[n:]
        copies = []
        if more:
            source, refs = refs[0], refs[1:]
        refs = refs[len(after) :]
        keeps, send, refs = refs[:n], refs[n], refs[n + 1 :]
        left = refs[more]
        if more:
            copies = coming.copies(source, refs[:more], refs[-1], me_ref[0], coming_chips)
        for copy in copies:
            copy.start()
        place(piece_refs, order, left)
        for i in range(n):
            for odd in (1, 0):
                out = dot(left[...], parts[i][odd], 1, 1 if by_rows else 0).astype(BF16)
                if odd:
                    send[i] = out
                else:
                    keeps[i][...] = out
        for copy in copies:
            copy.wait()

    outs = call(
        kernel,
        [("smem", weight.me)]
        + in_vmem(pieces)
        + in_vmem([weight.held[chip] for chip in chips])
        + ([("hbm", coming.value)] if more else []),
        [("vmem", ((tokens, block), BF16))] * n
        + [("vmem", ((n, tokens, block), BF16))]
        + ([("vmem", coming.shape())] * more if more else []),
        4 * tokens * weight.width * block * n,
        weight.moved(chips),
        after,
        [pltpu.VMEM((tokens, weight.width), BF16)]
        + ([pltpu.SemaphoreType.DMA((2 * more,))] if more else []),
    )
    if more:
        coming.held.update(zip(coming_chips, outs[n + 1 :]))
    return outs[:n], outs[n]


def block_sum(weight, stacks, odds, cols, groups, so_far=None, after=()):
    width, by_rows, block = weight.width, weight.by_rows, weight.block
    chips = len(weight.held)
    tokens = stacks[0].shape[0] // chips
    n, size = len(stacks), tokens // cols

    def kernel(*refs):
        stack_refs, parts, refs = refs[:n], refs[n : n + chips], refs[n + chips :]
        before, refs = (refs[0], refs[1:]) if so_far is not None else (None, refs)
        outs, total = refs[len(after) : -1], refs[-1]
        first = before is None
        if not first:
            total[...] = before[...]
        for i in range(chips):
            for stack, odd in zip(stack_refs, odds):
                value = stack[i * tokens : (i + 1) * tokens, :]
                term = dot(value, parts[i][odd], 1, 0 if by_rows else 1)
                total[...] = term if first else total[...] + term
                first = False
        if not groups:
            outs[0][...] = total[...]
        for group, out in zip(groups, outs):
            for i, q in enumerate(group):
                out[i * size : (i + 1) * size, :] = total[q * size : (q + 1) * size, :].astype(BF16)

    return call(
        kernel,
        in_vmem(stacks)
        + in_vmem([weight.held[chip] for chip in range(chips)])
        + in_vmem([so_far] if so_far is not None else []),
        [("vmem", ((len(group) * size, width), BF16)) for group in groups]
        or [("vmem", ((tokens, width), F32))],
        2 * tokens * width * block * chips * n,
        weight.moved(range(chips)) // 2 * n,
        after,
        [pltpu.VMEM((tokens, width), F32)],
    )


def weight_grad(weight, stacks, shards, after=()):
    pieces, order = shards
    chips, block = len(weight.held), weight.block
    rows, tokens = 2 * chips, stacks[0].shape[0] // chips
    width, by_rows = weight.width, weight.by_rows
    halves = 2
    size = (block if by_rows else width) // halves

    def kernel(me_ref, *refs):
        stack_refs, refs = refs[:2], refs[2:]
        piece_refs, refs = refs[: len(pieces)], refs[len(pieces) :]
        grad, other, ready, sent = refs[len(after) :]
        place(piece_refs, order, other)
        me = me_ref[0]

        def write(step):
            r, half = step // halves, step % halves
            to = weight.part(grad, me, r)
            to = to.at[half * size : (half + 1) * size, :]
            return pltpu.make_async_copy(ready.at[step % WRITES], to, sent.at[step % WRITES])

        steps = rows * halves
        for step in range(steps):
            r, half = step // halves, step % halves
            if step >= WRITES:
                write(step - WRITES).wait()
            stack, of = stack_refs[r % 2], slice(r // 2 * tokens, (r // 2 + 1) * tokens)
            at = slice(half * size, (half + 1) * size)
            if by_rows:
                out = dot(stack[of, at], other[...], 0, 0)
            else:
                out = dot(other[:, at], stack[of, :], 0, 0)
            ready[step % WRITES] = out.astype(BF16)
            write(step).start()
        for step in range(max(0, steps - WRITES), steps):
            write(step).wait()

    return call(
        kernel,
        [("smem", weight.me)] + in_vmem(stacks) + in_vmem(pieces),
        [("hbm", (weight.value.shape, BF16))],
        2 * tokens * width * block * rows,
        weight.moved(range(chips)),
        after,
        [
            pltpu.VMEM((tokens, width), BF16),
            pltpu.VMEM((WRITES, size, width if by_rows else block), BF16),
            pltpu.SemaphoreType.DMA((WRITES,)),
        ],
    )[0]


def activate(keep, got, travelled, after=()):
    def kernel(keep_ref, got_ref, *refs):
        total = keep_ref[...].astype(F32) + got_ref[0].astype(F32)
        for ref in refs[: len(travelled)]:
            total = total + ref[...].astype(F32)
        refs[-2][...] = total
        refs[-1][...] = gelu_fn(total).astype(BF16)

    shape = keep.shape
    return call(
        kernel,
        in_vmem([keep, got, *travelled]),
        [("vmem", (shape, F32)), ("vmem", (shape, BF16))],
        0,
        0,
        after,
    )


def activate_back(hidden, keep, got, travelled, after=()):
    def kernel(hidden_ref, keep_ref, got_ref, *refs):
        total = keep_ref[...].astype(F32) + got_ref[0].astype(F32)
        for ref in refs[: len(travelled)]:
            total = total + ref[...].astype(F32)
        refs[-1][...] = gelu_back(hidden_ref[...], total)

    return call(
        kernel, in_vmem([hidden, keep, got, *travelled]), [("vmem", (keep.shape, BF16))], 0, 0, after
    )[0]


def pair_sums(keeps, got, chips):
    return {
        chip: (keep.astype(F32) + got[i].astype(F32)).astype(BF16)
        for i, (chip, keep) in enumerate(zip(chips, keeps))
        if chip
    }


def gather_row(share, rows, after=()):
    own = [share] + [swap(share, "row", 2 * i, rows) for i in range(1, rows // 2)]
    stack = joined(own, after)
    return stack, swap(stack, "row", 1, rows)


def exchange_col(parts, cols):
    return [parts[0]] + [swap(parts[q], "col", q, cols) for q in range(cols - 1, 0, -1)]


def summed(parts):
    return sum(part.astype(F32) for part in parts).astype(BF16)


def blocked(rows, cols, tokens, cotangent, w_in, w_out):
    me = lax.axis_index("row").astype(jnp.int32).reshape(1)
    w_in, w_out = Weight(me, w_in, rows, False), Weight(me, w_out, rows, True)
    chips = list(range(rows // 2))
    far, near = chips[len(chips) // 2 :], chips[: len(chips) // 2]

    flips = [1 << bit for bit in range(cols.bit_length() - 1)]
    token_pieces, token_order = [tokens], [0]
    cot_pieces, cot_order = [cotangent], [0]
    load(w_in, far)
    token_sent, cot_sent = tokens, cotangent
    for hop in range(len(flips)):
        if hop:
            token_sent = joined(token_pieces, (cot_pieces[-1], w_in.held[far[0]]))
            cot_sent = joined(cot_pieces, (token_sent,))
        flip = flips[-1 - hop]
        token_pieces.append(swap(token_sent, "col", flip, cols))
        token_order += [q ^ flip for q in token_order]
        if hop and hop == len(flips) - 1:
            load(w_in, near, (token_sent,))
            cot_sent = joined([cot_sent], (token_pieces[-1], w_in.held[near[0]]))
        cot_pieces.append(swap(cot_sent, "col", flips[hop], cols))
        cot_order += [q ^ flips[hop] for q in cot_order]
    token_shards, cot_shards = (token_pieces, token_order), (cot_pieces, cot_order)

    def travel(pairs):
        return {chip: swap(pairs[chip], "row", 2 * chip, rows) for chip in pairs}

    far_keeps, send = project(w_in, token_shards, far, (cot_sent,), w_out, far[: len(far) // 2])
    far_got = swap(send, "row", 1, rows)
    near_keeps, send = project(w_in, token_shards, near, (send,), w_out, far[len(far) // 2 :])
    near_got = swap(send, "row", 1, rows)
    far_pairs = pair_sums(far_keeps, far_got, far)
    near_pairs = pair_sums(near_keeps, near_got, near)
    travelled = {**travel(far_pairs), **travel(near_pairs)}
    own = near_keeps[0], near_got, [travelled[chip] for chip in chips[:0:-1]]
    load(w_out, near, (*far_pairs.values(), *near_pairs.values()))

    far_keeps, send = project(
        w_out,
        cot_shards,
        far,
        (w_out.held[near[0]], *travelled.values()),
    )
    hidden, act = activate(*own, (send,))
    far_got = swap(send, "row", 1, rows)
    far_pairs = pair_sums(far_keeps, far_got, far)
    near_keeps, send = project(w_out, cot_shards, near, (act, *far_pairs.values()))
    near_got = swap(send, "row", 1, rows)
    near_pairs = pair_sums(near_keeps, near_got, near)
    travelled = {**travel(far_pairs), **travel(near_pairs)}
    back_own = near_keeps[0], near_got, [travelled[chip] for chip in chips[:0:-1]]

    act = gather_row(act, rows, (send,))
    even, odd = range(0, cols, 2), range(1, cols, 2)
    keep, send = block_sum(w_out, act, (0, 1), cols, (even, odd))
    grad_hidden = activate_back(hidden, *back_own, (keep,))
    got = swap(send, "col", 1, cols)
    sums = [
        half.astype(F32) + other.astype(F32)
        for half, other in zip(jnp.split(keep, len(even)), jnp.split(got, len(even)))
    ]
    layer_parts = [
        swap(part.astype(BF16), "col", q, cols) for part, q in zip(sums[:0:-1], even[:0:-1])
    ]
    grad_w_out = weight_grad(w_out, act, cot_shards, (got,))
    hbm_grad = pltpu.with_memory_space_constraint(grad_w_out, pltpu.HBM)
    grad_hidden = gather_row(grad_hidden, rows, (hbm_grad, *layer_parts))

    (so_far,) = block_sum(w_in, grad_hidden[:1], (0,), cols, ())
    token_parts = block_sum(w_in, grad_hidden[1:], (1,), cols, [[q] for q in range(cols)], so_far)
    grad_w_in = weight_grad(w_in, grad_hidden, token_shards, tuple(token_parts))
    token_parts = exchange_col(token_parts, cols)
    return (summed([sums[0], *layer_parts]), summed(token_parts), grad_w_in, grad_w_out)


def collective(tokens, cotangent, w_in, w_out):
    token_full = lax.all_gather(tokens, "col", axis=0, tiled=True)
    cot_full = lax.all_gather(cotangent, "col", axis=0, tiled=True)

    def over(value, axis):
        return lax.psum_scatter(value.astype(BF16), axis, scatter_dimension=0, tiled=True)

    hidden = over(dot(token_full, w_in, 1, 0), "row").astype(F32)
    grad_act = over(dot(cot_full, w_out, 1, 1), "row").astype(F32)
    act = lax.all_gather(gelu_fn(hidden).astype(BF16), "row", axis=0, tiled=True)
    grad_hidden = lax.all_gather(gelu_back(hidden, grad_act), "row", axis=0, tiled=True)
    layer_out = over(dot(act, w_out, 1, 0), "col")
    grad_tokens = over(dot(grad_hidden, w_in, 1, 1), "col")
    grad_w_in = dot(token_full, grad_hidden, 0, 0).astype(BF16)
    grad_w_out = dot(act, cot_full, 0, 0).astype(BF16)
    return (layer_out, grad_tokens, grad_w_in, grad_w_out)


def solution(mesh):
    rows, cols = mesh.shape["row"], mesh.shape["col"]

    def shards(tokens, cotangent, w_in, w_out):
        powers = rows & (rows - 1) == 0 and cols & (cols - 1) == 0
        if powers and rows > 2 and cols > 1 and w_in.shape[1] % (rows * 128) == 0:
            return blocked(rows, cols, tokens, cotangent, w_in, w_out)
        return collective(tokens, cotangent, w_in, w_out)

    return jax.shard_map(
        shards,
        mesh=mesh,
        in_specs=(P("col", "row"), P("col", "row"), P("row", "col"), P("col", "row")),
        out_specs=(P("col", "row"), P("col", "row"), P("row", "col"), P("col", "row")),
        check_vma=False,
    )
```

time: 254 us -> 102 us (0.40)
  waiting for transfers between devices: 112 us -> 14.8 us
  matrix products: 68 us -> 0 us
  Pallas kernels: 0 us -> 52.1 us
  starting transfers between devices: 0.42 us -> 32.6 us
  blocking collectives: 31.9 us -> 0 us
  local copies, waits for them, and re-layouts: 24.7 us -> 0.01 us
  between operations: 14.1 us -> 0.93 us
    reduce_scatter x4 -> x0, waiting for transfers between devices: 68.3 us -> none  [the longest x1 42.4 us: shards(): lax.psum_scatter(jnp.dot(block, w_in, preferred_element_type=jnp.float32)...]
    dot_general x6 -> x0, matrix products: 68 us -> none  [the longest x1 13.7 us: shards(): lax.dot_general(block, w_out, (((1,), (1,)), ((), ())), preferred_element...]
    pallas_call x0 -> x19, Pallas kernels: none -> 52.1 us  [call(): pl.pallas_call(kernel, in_specs=[pl.BlockSpec(memory_space=spaces[space])...]
    all_gather x2 -> x0, waiting for transfers between devices: 43 us -> none  [the longest x1 25.4 us: shards(): act = lax.all_gather(act_share, 'row', axis=0, tiled=True)]
    ppermute x0 -> x27, starting transfers between devices: none -> 32.6 us  [swap(): return lax.ppermute(value, axis, [(i, i ^ flip) for i in range(count)])]
    all_gather x2 -> x0, blocking collectives: 31.9 us -> none  [the longest x1 16.4 us: shards(): lax.all_gather(cotangent, 'col', axis=0, tiled=True)]
    unnamed x7 -> x4, local copies, waits for them, and re-layouts: 24.7 us -> 0.01 us
    ppermute x0 -> x27, waiting for transfers between devices: none -> 14.8 us  [swap(): return lax.ppermute(value, axis, [(i, i ^ flip) for i in range(count)])]
  transfers between devices with their start and end apart: 6 -> 27, of which waited for: 5 -> 9; matrix products, arithmetic and copies ran while one was open for 31% -> 1% of each run, Pallas kernels for 0% -> 41%
where the time goes in v3:
time: 102 us
  Pallas kernels  52.1 us (51%)
  starting transfers between devices  32.6 us (32%)
  waiting for transfers between devices  14.8 us (15%)
  other arithmetic  1.68 us (2%)
    pallas_call x19, Pallas kernels, call(): pl.pallas_call(kernel, in_specs=[pl.BlockSpec(memory_space=spaces[space])...  52.1 us
    ppermute x27, starting transfers between devices, swap(): return lax.ppermute(value, axis, [(i, i ^ flip) for i in range(count)])  32.6 us
    ppermute x27, waiting for transfers between devices, swap(): return lax.ppermute(value, axis, [(i, i ^ flip) for i in range(count)])  14.8 us
  transfers between devices with their start and end apart: 27, of which 9 were waited for; matrix products, arithmetic and copies ran while one was open for 1% of the time, Pallas kernels for 41%

profile of v3, /device:TPU:0, one launch (start us, length us, event | category | flops | bytes accessed | tf_op | source)
XLA Modules:
  0.0 102.1 jit_solution(5934138976748077413)
XLA Ops:
  0.6 4.1 %collective-permute-start = (bf16[32,1536]{1,0:T(8,128)(2,1)}, bf16[32,1536]{1,0:T(8,128)(2,1)S(1)}, u32[]{:S(2)}, u32[]{:S(2)}) collective-permute-start(bf16[32,1536]{1,0:T(8,128)(2,1)} %refs_2_.3), channel_id=1, source_target_pairs={{0,2},{1,3},{2,0},{3,1},{4,6},{5,7},{6,4},{7,5},{8,10},{9,11},{10,... | collective-permute-start | bytes 294920 | tf_op jit(solution)/shard_map/ppermute | solution.py:26
  6.3 3.9 %shard_map.75 = (bf16[2,1536,768]{2,1,0:T(8,128)(2,1)S(1)}, bf16[2,1536,768]{2,1,0:T(8,128)(2,1)S(1)}) custom-call(s32[1]{0:T(128)} %bitcast.me_ref, bf16[1536,6144]{1,0:T(8,128)(2,1)} %source.4), custom_call_target="tpu_custom_call" | custom-call | tf_op jit(solution)/shard_map/pallas_call | solution.py:44
  11.8 3.8 %shard_map.77 = (bf16[2,1536,768]{2,1,0:T(8,128)(2,1)S(1)}, bf16[2,1536,768]{2,1,0:T(8,128)(2,1)S(1)}) custom-call(s32[1]{0:T(128)} %bitcast.me_ref, bf16[1536,6144]{1,0:T(8,128)(2,1)} %source.4, bf16[64,1536]{1,0:T(8,128)(2,1)S(1)} %shard_map.76.refs_0_.refs_2_), custom_call_target="tpu_custom_call" | custom-call | tf_op jit(solution)/shard_map/pallas_call | solution.py:44
  16.4 3.6 %shard_map.80 = (bf16[128,768]{1,0:T(8,128)(2,1)S(1)}, bf16[128,768]{1,0:T(8,128)(2,1)S(1)}, bf16[2,128,768]{2,1,0:T(8,128)(2,1)S(1)}, bf16[2,768,1536]{2,1,0:T(8,128)(2,1)S(1)}) custom-call(s32[1]{0:T(128)} %bitcast.me_ref, bf16[32,1536]{1,0:T(8,128)(2,1)S(1)} %copy-done.1, bf16[32,1536]{1,0:T(8,128)(2,1)S(1)} %collective-permute-done.refs_1_.refs_3_, ...), custom_call_target="tpu_custom_call" | custom-call | flops 1207959552 | bytes 9437184 | tf_op jit(solution)/shard_map/pallas_call | solution.py:44
  20.1 3.6 %shard_map.81 = (bf16[128,768]{1,0:T(8,128)(2,1)S(1)}, bf16[128,768]{1,0:T(8,128)(2,1)S(1)}, bf16[2,128,768]{2,1,0:T(8,128)(2,1)S(1)}, bf16[2,768,1536]{2,1,0:T(8,128)(2,1)S(1)}) custom-call(s32[1]{0:T(128)} %bitcast.me_ref, bf16[32,1536]{1,0:T(8,128)(2,1)S(1)} %copy-done.1, bf16[32,1536]{1,0:T(8,128)(2,1)S(1)} %collective-permute-done.refs_1_.refs_3_, ...), custom_call_target="tpu_custom_call" | custom-call | flops 1207959552 | bytes 9437184 | tf_op jit(solution)/shard_map/pallas_call | solution.py:44
  24.3 2.7 %collective-permute-start.8 = (bf16[64,1536]{1,0:T(8,128)(2,1)S(1)}, bf16[64,1536]{1,0:T(8,128)(2,1)S(1)}, u32[]{:S(2)}, u32[]{:S(2)}) collective-permute-start(bf16[64,1536]{1,0:T(8,128)(2,1)S(1)} %shard_map.79.refs_6_), channel_id=1, source_target_pairs={{0,2},{1,3},{2,0},{3,1},{4,6},{5,7},{6,4},{7,5},{8,10},{9,11},{10,... | collective-permute-start | bytes 589832 | tf_op jit(solution)/shard_map/ppermute | solution.py:26
  30.8 3.8 %shard_map.82 = (bf16[2,768,1536]{2,1,0:T(8,128)(2,1)S(1)}, bf16[2,768,1536]{2,1,0:T(8,128)(2,1)S(1)}) custom-call(s32[1]{0:T(128)} %bitcast.me_ref, bf16[6144,1536]{1,0:T(8,128)(2,1)} %source.5, bf16[128,768]{1,0:T(8,128)(2,1)S(1)} %get-tuple-element.62.refs_0_, bf16[128,768]{1,0:T(8,128)(2,1)S(1)} %get-tuple-element.63.refs_1_, ...), custom_call_target="tpu_custom_call" | custom-call | tf_op jit(solution)/shard_map/pallas_call | solution.py:44
  34.6 1.8 %collective-permute-done.8.refs_2_.refs_4_ = bf16[64,1536]{1,0:T(8,128)(2,1)S(1)} collective-permute-done((bf16[64,1536]{1,0:T(8,128)(2,1)S(1)}, bf16[64,1536]{1,0:T(8,128)(2,1)S(1)}, u32[]{:S(2)}, u32[]{:S(2)}) %collective-permute-start.8) | collective-permute-done | bytes 196640 | tf_op jit(solution)/shard_map/ppermute | solution.py:26
  36.4 1.6 %collective-permute-done.6.refs_6_.refs_1_ = bf16[128,768]{1,0:T(8,128)(2,1)S(1)} collective-permute-done((bf16[128,768]{1,0:T(8,128)(2,1)S(1)}, bf16[128,768]{1,0:T(8,128)(2,1)S(1)}, u32[]{:S(2)}, u32[]{:S(2)}) %collective-permute-start.6) | collective-permute-done | bytes 196640 | tf_op jit(solution)/shard_map/ppermute | solution.py:26
  39.3 3.1 %shard_map.83 = (bf16[128,768]{1,0:T(8,128)(2,1)S(1)}, bf16[128,768]{1,0:T(8,128)(2,1)S(1)}, bf16[2,128,768]{2,1,0:T(8,128)(2,1)S(1)}) custom-call(s32[1]{0:T(128)} %bitcast.me_ref, bf16[32,1536]{1,0:T(8,128)(2,1)S(1)} %copy-done, bf16[32,1536]{1,0:T(8,128)(2,1)S(1)} %collective-permute-done.1.refs_2_.refs_1_.refs_3_, ...), custom_call_target="tpu_custom_call" | custom-call | flops 1207959552 | bytes 9437184 | tf_op jit(solution)/shard_map/pallas_call | solution.py:44
  42.7 2.5 %collective-permute-start.11 = (bf16[128,768]{1,0:T(8,128)(2,1)S(1)}, bf16[128,768]{1,0:T(8,128)(2,1)S(1)}, u32[]{:S(2)}, u32[]{:S(2)}) collective-permute-start(bf16[128,768]{1,0:T(8,128)(2,1)S(1)} %get-tuple-element.46.refs_5_.refs_0_), channel_id=1, source_target_pairs={{0,24},{4,28},{8,16},{12,20},{16,8},{20,12},{24,0},{28,4},{1,25},{... | collective-permute-start | bytes 589832 | tf_op jit(solution)/shard_map/ppermute | solution.py:26
  46.4 3.2 %shard_map.85 = (bf16[128,768]{1,0:T(8,128)(2,1)S(1)}, bf16[128,768]{1,0:T(8,128)(2,1)S(1)}, bf16[2,128,768]{2,1,0:T(8,128)(2,1)S(1)}) custom-call(s32[1]{0:T(128)} %bitcast.me_ref, bf16[32,1536]{1,0:T(8,128)(2,1)S(1)} %copy-done, bf16[32,1536]{1,0:T(8,128)(2,1)S(1)} %collective-permute-done.1.refs_2_.refs_1_.refs_3_, ...), custom_call_target="tpu_custom_call" | custom-call | flops 1207959552 | bytes 9437184 | tf_op jit(solution)/shard_map/pallas_call | solution.py:44
  49.6 1.9 %collective-permute-done.11.refs_3_ = bf16[128,768]{1,0:T(8,128)(2,1)S(1)} collective-permute-done((bf16[128,768]{1,0:T(8,128)(2,1)S(1)}, bf16[128,768]{1,0:T(8,128)(2,1)S(1)}, u32[]{:S(2)}, u32[]{:S(2)}) %collective-permute-start.11) | collective-permute-done | bytes 196640 | tf_op jit(solution)/shard_map/ppermute | solution.py:26
  51.5 3.8 %collective-permute-done.10.refs_2_ = bf16[128,768]{1,0:T(8,128)(2,1)S(1)} collective-permute-done((bf16[128,768]{1,0:T(8,128)(2,1)S(1)}, bf16[128,768]{1,0:T(8,128)(2,1)S(1)}, u32[]{:S(2)}, u32[]{:S(2)}) %collective-permute-start.10) | collective-permute-done | bytes 196640 | tf_op jit(solution)/shard_map/ppermute | solution.py:26
  56.0 1.7 %collective-permute-start.17 = (bf16[128,768]{1,0:T(8,128)(2,1)S(1)}, bf16[128,768]{1,0:T(8,128)(2,1)S(1)}, u32[]{:S(2)}, u32[]{:S(2)}) collective-permute-start(bf16[128,768]{1,0:T(8,128)(2,1)S(1)} %get-tuple-element.60.refs_7_), channel_id=1, source_target_pairs={{0,24},{4,28},{8,16},{12,20},{16,8},{20,12},{24,0},{28,4},{1,25},{... | collective-permute-start | bytes 589832 | tf_op jit(solution)/shard_map/ppermute | solution.py:26
  59.9 2.6 %shard_map.87 = (bf16[64,1536]{1,0:T(8,128)(2,1)S(1)}, bf16[64,1536]{1,0:T(8,128)(2,1)S(1)}) custom-call(bf16[512,768]{1,0:T(8,128)(2,1)S(1)} %shard_map.86.refs_0_, bf16[512,768]{1,0:T(8,128)(2,1)S(1)} %collective-permute-done.13.refs_1_, bf16[2,768,1536]{2,1,0:T(8,128)(2,1)S(1)} %get-tuple-element.44.refs_5_.refs_3_.refs_2_, ...), custom_call_target="tpu_custom_call" | custom-call | flops 2415919104 | bytes 18874368 | tf_op jit(solution)/shard_map/pallas_call | solution.py:44
  62.5 1.8 %collective-permute-start.14 = (bf16[64,1536]{1,0:T(8,128)(2,1)S(1)}, bf16[64,1536]{1,0:T(8,128)(2,1)S(1)}, u32[]{:S(2)}, u32[]{:S(2)}) collective-permute-start(bf16[64,1536]{1,0:T(8,128)(2,1)S(1)} %get-tuple-element.52), channel_id=1, source_target_pairs={{0,1},{1,0},{2,3},{3,2},{4,5},{5,4},{6,7},{7,6},{8,9},{9,8},{10,11... | collective-permute-start | bytes 589832 | tf_op jit(solution)/shard_map/ppermute | solution.py:26
  64.7 3.3 %collective-permute-done.18.refs_1_ = bf16[128,768]{1,0:T(8,128)(2,1)S(1)} collective-permute-done((bf16[128,768]{1,0:T(8,128)(2,1)S(1)}, bf16[128,768]{1,0:T(8,128)(2,1)S(1)}, u32[]{:S(2)}, u32[]{:S(2)}) %collective-permute-start.18) | collective-permute-done | bytes 196640 | tf_op jit(solution)/shard_map/ppermute | solution.py:26
  68.4 1.7 %collective-permute-start.22 = (bf16[128,768]{1,0:T(8,128)(2,1)S(1)}, bf16[128,768]{1,0:T(8,128)(2,1)S(1)}, u32[]{:S(2)}, u32[]{:S(2)}) collective-permute-start(bf16[128,768]{1,0:T(8,128)(2,1)S(1)} %shard_map.88.refs_0_), channel_id=1, source_target_pairs={{0,24},{4,28},{8,16},{12,20},{16,8},{20,12},{24,0},{28,4},{1,25},{... | collective-permute-start | bytes 589832 | tf_op jit(solution)/shard_map/ppermute | solution.py:26
  72.3 8.3 %shard_map.89.refs_4_ = bf16[6144,1536]{1,0:T(8,128)(2,1)} custom-call(s32[1]{0:T(128)} %bitcast.me_ref, bf16[512,768]{1,0:T(8,128)(2,1)S(1)} %shard_map.86.refs_0_, bf16[512,768]{1,0:T(8,128)(2,1)S(1)} %collective-permute-done.13.refs_1_, bf16[32,1536]{1,0:T(8,128)(2,1)S(1)} %copy-done, bf16[32,1536]{1,0:T(8,128)(2,1)S(1)} %collective-permute-done.1.refs_2_.refs_1_.refs_3_, ...), custom_call_target="tpu_custom_call" | custom-call | flops 2415919104 | bytes 18874368 | tf_op jit(solution)/shard_map/pallas_call | solution.py:44
  80.8 3.1 %shard_map.91.refs_5_ = f32[128,1536]{1,0:T(8,128)S(1)} custom-call(bf16[512,768]{1,0:T(8,128)(2,1)S(1)} %shard_map.90.refs_0_, bf16[2,1536,768]{2,1,0:T(8,128)(2,1)S(1)} %get-tuple-element.33.refs_2_.refs_3_.refs_1_, bf16[2,1536,768]{2,1,0:T(8,128)(2,1)S(1)} %get-tuple-element.34.refs_4_.refs_2_, bf16[2,1536,768]{2,1,0:T(8,128)(2,1)S(1)} %get-tuple-element.32.refs_3_, ...), custom_call_target="tpu_custom_call" | custom-call | flops 1207959552 | bytes 9437184 | tf_op jit(solution)/shard_map/pallas_call | solution.py:44
  84.6 3.1 %shard_map.92 = (bf16[32,1536]{1,0:T(8,128)(2,1)S(1)}, bf16[32,1536]{1,0:T(8,128)(2,1)S(1)}, bf16[32,1536]{1,0:T(8,128)(2,1)S(1)}, bf16[32,1536]{1,0:T(8,128)(2,1)S(1)}) custom-call(bf16[512,768]{1,0:T(8,128)(2,1)S(1)} %collective-permute-done.23.refs_0_.refs_1_, bf16[2,1536,768]{2,1,0:T(8,128)(2,1)S(1)} %get-tuple-element.33.refs_2_.refs_3_.refs_1_, ...), custom_call_target="tpu_custom_call" | custom-call | flops 1207959552 | bytes 9437184 | tf_op jit(solution)/shard_map/pallas_call | solution.py:44
  87.7 3.9 %collective-permute-start.24 = (bf16[32,1536]{1,0:T(8,128)(2,1)S(1)}, bf16[32,1536]{1,0:T(8,128)(2,1)S(1)}, u32[]{:S(2)}, u32[]{:S(2)}) collective-permute-start(bf16[32,1536]{1,0:T(8,128)(2,1)S(1)} %get-tuple-element.57.refs_8_), channel_id=1, source_target_pairs={{0,3},{1,2},{2,1},{3,0},{4,7},{5,6},{6,5},{7,4},{8,11},{9,10},{10,... | collective-permute-start | bytes 294920 | tf_op jit(solution)/shard_map/ppermute | solution.py:26
  92.2 9.2 %shard_map.93 = bf16[1536,6144]{1,0:T(8,128)(2,1)} custom-call(s32[1]{0:T(128)} %bitcast.me_ref, bf16[512,768]{1,0:T(8,128)(2,1)S(1)} %shard_map.90.refs_0_, bf16[512,768]{1,0:T(8,128)(2,1)S(1)} %collective-permute-done.23.refs_0_.refs_1_, bf16[32,1536]{1,0:T(8,128)(2,1)S(1)} %copy-done.1, bf16[32,1536]{1,0:T(8,128)(2,1)S(1)} %collective-permute-done.refs_1_.refs_3_, ...), custom_call_target="tpu_custom_call" | custom-call | flops 2415919104 | bytes 18874368 | tf_op jit(solution)/shard_map/pallas_call | solution.py:44
  (60 shorter events, 19.1 us)
Async XLA Ops:
  0.6 9.6 %collective-permute-start = (bf16[32,1536]{1,0:T(8,128)(2,1)}, bf16[32,1536]{1,0:T(8,128)(2,1)S(1)}, u32[]{:S(2)}, u32[]{:S(2)}) collective-permute-start(bf16[32,1536]{1,0:T(8,128)(2,1)} %refs_2_.3), channel_id=1, source_target_pairs={{0,2},{1,3},{2,0},{3,1},{4,6},{5,7},{6,4},{7,5},{8,10},{9,11},{10,... | collective-permute-start | bytes 294920 | tf_op jit(solution)/shard_map/ppermute | solution.py:26
  4.7 5.5 %collective-permute-start.1 = (bf16[32,1536]{1,0:T(8,128)(2,1)}, bf16[32,1536]{1,0:T(8,128)(2,1)S(1)}, u32[]{:S(2)}, u32[]{:S(2)}) collective-permute-start(bf16[32,1536]{1,0:T(8,128)(2,1)} %refs_2_.2), channel_id=1, source_target_pairs={{0,1},{1,0},{2,3},{3,2},{4,5},{5,4},{6,7},{7,6},{8,9},{9,8},{10,11... | collective-permute-start | bytes 294920 | tf_op jit(solution)/shard_map/ppermute | solution.py:26
  10.2 6.1 %collective-permute-start.2 = (bf16[64,1536]{1,0:T(8,128)(2,1)S(1)}, bf16[64,1536]{1,0:T(8,128)(2,1)S(1)}, u32[]{:S(2)}, u32[]{:S(2)}) collective-permute-start(bf16[64,1536]{1,0:T(8,128)(2,1)S(1)} %shard_map.76.refs_0_.refs_2_), channel_id=1, source_target_pairs={{0,1},{1,0},{2,3},{3,2},{4,5},{5,4},{6,7},{7,6},{8,9},{9,8},{10,11... | collective-permute-start | bytes 589832 | tf_op jit(solution)/shard_map/ppermute | solution.py:26
  20.0 7.0 %collective-permute-start.4 = (bf16[2,128,768]{2,1,0:T(8,128)(2,1)S(1)}, bf16[2,128,768]{2,1,0:T(8,128)(2,1)S(1)}, u32[]{:S(2)}, u32[]{:S(2)}) collective-permute-start(bf16[2,128,768]{2,1,0:T(8,128)(2,1)S(1)} %get-tuple-element.36.refs_6_), channel_id=1, source_target_pairs={{0,4},{4,0},{8,12},{12,8},{16,20},{20,16},{24,28},{28,24},{1,5},{5... | collective-permute-start | bytes 1179656 | tf_op jit(solution)/shard_map/ppermute | solution.py:26
  23.7 6.4 %collective-permute-start.3 = (bf16[2,128,768]{2,1,0:T(8,128)(2,1)S(1)}, bf16[2,128,768]{2,1,0:T(8,128)(2,1)S(1)}, u32[]{:S(2)}, u32[]{:S(2)}) collective-permute-start(bf16[2,128,768]{2,1,0:T(8,128)(2,1)S(1)} %get-tuple-element.38), channel_id=1, source_target_pairs={{0,4},{4,0},{8,12},{12,8},{16,20},{20,16},{24,28},{28,24},{1,5},{5... | collective-permute-start | bytes 1179656 | tf_op jit(solution)/shard_map/ppermute | solution.py:26
  24.3 12.1 %collective-permute-start.8 = (bf16[64,1536]{1,0:T(8,128)(2,1)S(1)}, bf16[64,1536]{1,0:T(8,128)(2,1)S(1)}, u32[]{:S(2)}, u32[]{:S(2)}) collective-permute-start(bf16[64,1536]{1,0:T(8,128)(2,1)S(1)} %shard_map.79.refs_6_), channel_id=1, source_target_pairs={{0,2},{1,3},{2,0},{3,1},{4,6},{5,7},{6,4},{7,5},{8,10},{9,11},{10,... | collective-permute-start | bytes 589832 | tf_op jit(solution)/shard_map/ppermute | solution.py:26
  27.1 10.9 %collective-permute-start.6 = (bf16[128,768]{1,0:T(8,128)(2,1)S(1)}, bf16[128,768]{1,0:T(8,128)(2,1)S(1)}, u32[]{:S(2)}, u32[]{:S(2)}) collective-permute-start(bf16[128,768]{1,0:T(8,128)(2,1)S(1)} %get-tuple-element.62.refs_0_), channel_id=1, source_target_pairs={{0,16},{4,20},{8,24},{12,28},{16,0},{20,4},{24,8},{28,12},{1,17},{... | collective-permute-start | bytes 589832 | tf_op jit(solution)/shard_map/ppermute | solution.py:26
  28.7 9.3 %collective-permute-start.5 = (bf16[128,768]{1,0:T(8,128)(2,1)S(1)}, bf16[128,768]{1,0:T(8,128)(2,1)S(1)}, u32[]{:S(2)}, u32[]{:S(2)}) collective-permute-start(bf16[128,768]{1,0:T(8,128)(2,1)S(1)} %get-tuple-element.63.refs_1_), channel_id=1, source_target_pairs={{0,24},{4,28},{8,16},{12,20},{16,8},{20,12},{24,0},{28,4},{1,25},{... | collective-permute-start | bytes 589832 | tf_op jit(solution)/shard_map/ppermute | solution.py:26
  30.2 9.0 %collective-permute-start.7 = (bf16[128,768]{1,0:T(8,128)(2,1)S(1)}, bf16[128,768]{1,0:T(8,128)(2,1)S(1)}, u32[]{:S(2)}, u32[]{:S(2)}) collective-permute-start(bf16[128,768]{1,0:T(8,128)(2,1)S(1)} %fusion.3.refs_2_), channel_id=1, source_target_pairs={{0,8},{4,12},{8,0},{12,4},{16,24},{20,28},{24,16},{28,20},{1,9},{5... | collective-permute-start | bytes 589832 | tf_op jit(solution)/shard_map/ppermute | solution.py:26
  42.7 8.7 %collective-permute-start.11 = (bf16[128,768]{1,0:T(8,128)(2,1)S(1)}, bf16[128,768]{1,0:T(8,128)(2,1)S(1)}, u32[]{:S(2)}, u32[]{:S(2)}) collective-permute-start(bf16[128,768]{1,0:T(8,128)(2,1)S(1)} %get-tuple-element.46.refs_5_.refs_0_), channel_id=1, source_target_pairs={{0,24},{4,28},{8,16},{12,20},{16,8},{20,12},{24,0},{28,4},{1,25},{... | collective-permute-start | bytes 589832 | tf_op jit(solution)/shard_map/ppermute | solution.py:26
  45.3 10.0 %collective-permute-start.10 = (bf16[128,768]{1,0:T(8,128)(2,1)S(1)}, bf16[128,768]{1,0:T(8,128)(2,1)S(1)}, u32[]{:S(2)}, u32[]{:S(2)}) collective-permute-start(bf16[128,768]{1,0:T(8,128)(2,1)S(1)} %get-tuple-element.46.refs_5_.refs_0_), channel_id=1, source_target_pairs={{0,16},{4,20},{8,24},{12,28},{16,0},{20,4},{24,8},{28,12},{1,17},{... | collective-permute-start | bytes 589832 | tf_op jit(solution)/shard_map/ppermute | solution.py:26
  45.8 9.6 %collective-permute-start.9 = (bf16[128,768]{1,0:T(8,128)(2,1)S(1)}, bf16[128,768]{1,0:T(8,128)(2,1)S(1)}, u32[]{:S(2)}, u32[]{:S(2)}) collective-permute-start(bf16[128,768]{1,0:T(8,128)(2,1)S(1)} %get-tuple-element.46.refs_5_.refs_0_), channel_id=1, source_target_pairs={{0,8},{4,12},{8,0},{12,4},{16,24},{20,28},{24,16},{28,20},{1,9},{5... | collective-permute-start | bytes 589832 | tf_op jit(solution)/shard_map/ppermute | solution.py:26
  55.4 4.5 %collective-permute-start.13 = (bf16[512,768]{1,0:T(8,128)(2,1)S(1)}, bf16[512,768]{1,0:T(8,128)(2,1)S(1)}, u32[]{:S(2)}, u32[]{:S(2)}) collective-permute-start(bf16[512,768]{1,0:T(8,128)(2,1)S(1)} %shard_map.86.refs_0_), channel_id=1, source_target_pairs={{0,4},{4,0},{8,12},{12,8},{16,20},{20,16},{24,28},{28,24},{1,5},{5... | collective-permute-start | bytes 2359304 | tf_op jit(solution)/shard_map/ppermute | solution.py:26
  56.0 8.7 %collective-permute-start.17 = (bf16[128,768]{1,0:T(8,128)(2,1)S(1)}, bf16[128,768]{1,0:T(8,128)(2,1)S(1)}, u32[]{:S(2)}, u32[]{:S(2)}) collective-permute-start(bf16[128,768]{1,0:T(8,128)(2,1)S(1)} %get-tuple-element.60.refs_7_), channel_id=1, source_target_pairs={{0,24},{4,28},{8,16},{12,20},{16,8},{20,12},{24,0},{28,4},{1,25},{... | collective-permute-start | bytes 589832 | tf_op jit(solution)/shard_map/ppermute | solution.py:26
  57.6 10.3 %collective-permute-start.18 = (bf16[128,768]{1,0:T(8,128)(2,1)S(1)}, bf16[128,768]{1,0:T(8,128)(2,1)S(1)}, u32[]{:S(2)}, u32[]{:S(2)}) collective-permute-start(bf16[128,768]{1,0:T(8,128)(2,1)S(1)} %get-tuple-element.61.refs_6_), channel_id=1, source_target_pairs={{0,16},{4,20},{8,24},{12,28},{16,0},{20,4},{24,8},{28,12},{1,17},{... | collective-permute-start | bytes 589832 | tf_op jit(solution)/shard_map/ppermute | solution.py:26
  59.0 9.0 %collective-permute-start.19 = (bf16[128,768]{1,0:T(8,128)(2,1)S(1)}, bf16[128,768]{1,0:T(8,128)(2,1)S(1)}, u32[]{:S(2)}, u32[]{:S(2)}) collective-permute-start(bf16[128,768]{1,0:T(8,128)(2,1)S(1)} %fusion), channel_id=1, source_target_pairs={{0,8},{4,12},{8,0},{12,4},{16,24},{20,28},{24,16},{28,20},{1,9},{5... | collective-permute-start | bytes 589832 | tf_op jit(solution)/shard_map/ppermute | solution.py:26
  62.5 9.4 %collective-permute-start.14 = (bf16[64,1536]{1,0:T(8,128)(2,1)S(1)}, bf16[64,1536]{1,0:T(8,128)(2,1)S(1)}, u32[]{:S(2)}, u32[]{:S(2)}) collective-permute-start(bf16[64,1536]{1,0:T(8,128)(2,1)S(1)} %get-tuple-element.52), channel_id=1, source_target_pairs={{0,1},{1,0},{2,3},{3,2},{4,5},{5,4},{6,7},{7,6},{8,9},{9,8},{10,11... | collective-permute-start | bytes 589832 | tf_op jit(solution)/shard_map/ppermute | solution.py:26
  68.4 12.2 %collective-permute-start.22 = (bf16[128,768]{1,0:T(8,128)(2,1)S(1)}, bf16[128,768]{1,0:T(8,128)(2,1)S(1)}, u32[]{:S(2)}, u32[]{:S(2)}) collective-permute-start(bf16[128,768]{1,0:T(8,128)(2,1)S(1)} %shard_map.88.refs_0_), channel_id=1, source_target_pairs={{0,24},{4,28},{8,16},{12,20},{16,8},{20,12},{24,0},{28,4},{1,25},{... | collective-permute-start | bytes 589832 | tf_op jit(solution)/shard_map/ppermute | solution.py:26
  70.1 10.5 %collective-permute-start.21 = (bf16[128,768]{1,0:T(8,128)(2,1)S(1)}, bf16[128,768]{1,0:T(8,128)(2,1)S(1)}, u32[]{:S(2)}, u32[]{:S(2)}) collective-permute-start(bf16[128,768]{1,0:T(8,128)(2,1)S(1)} %shard_map.88.refs_0_), channel_id=1, source_target_pairs={{0,16},{4,20},{8,24},{12,28},{16,0},{20,4},{24,8},{28,12},{1,17},{... | collective-permute-start | bytes 589832 | tf_op jit(solution)/shard_map/ppermute | solution.py:26
  71.4 9.2 %collective-permute-start.20 = (bf16[128,768]{1,0:T(8,128)(2,1)S(1)}, bf16[128,768]{1,0:T(8,128)(2,1)S(1)}, u32[]{:S(2)}, u32[]{:S(2)}) collective-permute-start(bf16[128,768]{1,0:T(8,128)(2,1)S(1)} %shard_map.88.refs_0_), channel_id=1, source_target_pairs={{0,8},{4,12},{8,0},{12,4},{16,24},{20,28},{24,16},{28,20},{1,9},{5... | collective-permute-start | bytes 589832 | tf_op jit(solution)/shard_map/ppermute | solution.py:26
  71.9 8.7 %collective-permute-start.15 = (bf16[32,1536]{1,0:T(8,128)(2,1)S(1)}, bf16[32,1536]{1,0:T(8,128)(2,1)S(1)}, u32[]{:S(2)}, u32[]{:S(2)}) collective-permute-start(bf16[32,1536]{1,0:T(8,128)(2,1)S(1)} %add_convert_fusion.2), channel_id=1, source_target_pairs={{0,2},{1,3},{2,0},{3,1},{4,6},{5,7},{6,4},{7,5},{8,10},{9,11},{10,... | collective-permute-start | bytes 294920 | tf_op jit(solution)/shard_map/ppermute | solution.py:26
  87.7 13.7 %collective-permute-start.24 = (bf16[32,1536]{1,0:T(8,128)(2,1)S(1)}, bf16[32,1536]{1,0:T(8,128)(2,1)S(1)}, u32[]{:S(2)}, u32[]{:S(2)}) collective-permute-start(bf16[32,1536]{1,0:T(8,128)(2,1)S(1)} %get-tuple-element.57.refs_8_), channel_id=1, source_target_pairs={{0,3},{1,2},{2,1},{3,0},{4,7},{5,6},{6,5},{7,4},{8,11},{9,10},{10,... | collective-permute-start | bytes 294920 | tf_op jit(solution)/shard_map/ppermute | solution.py:26
  91.5 9.8 %collective-permute-start.25 = (bf16[32,1536]{1,0:T(8,128)(2,1)S(1)}, bf16[32,1536]{1,0:T(8,128)(2,1)S(1)}, u32[]{:S(2)}, u32[]{:S(2)}) collective-permute-start(bf16[32,1536]{1,0:T(8,128)(2,1)S(1)} %get-tuple-element.58.refs_7_), channel_id=1, source_target_pairs={{0,2},{1,3},{2,0},{3,1},{4,6},{5,7},{6,4},{7,5},{8,10},{9,11},{10,... | collective-permute-start | bytes 294920 | tf_op jit(solution)/shard_map/ppermute | solution.py:26
  91.5 9.8 %collective-permute-start.26 = (bf16[32,1536]{1,0:T(8,128)(2,1)S(1)}, bf16[32,1536]{1,0:T(8,128)(2,1)S(1)}, u32[]{:S(2)}, u32[]{:S(2)}) collective-permute-start(bf16[32,1536]{1,0:T(8,128)(2,1)S(1)} %get-tuple-element.59.refs_6_), channel_id=1, source_target_pairs={{0,1},{1,0},{2,3},{3,2},{4,5},{5,4},{6,7},{7,6},{8,9},{9,8},{10,11... | collective-permute-start | bytes 294920 | tf_op jit(solution)/shard_map/ppermute | solution.py:26
  (5 other events, 20.5 us)
